TPU v7x, 256 devices: a whole 4x4x8 slice. The times are simulated.
256 devices in a mesh: seq: 32 (over z, x), dp: 8 (over y, core).
Axes of the slice: x: 4, y: 4, z: 8, core: 2. Of those that a mesh axis runs over, the one named last changes fastest.
Arguments:
- queries: bfloat16 [8, 12288, 1536], P('dp', 'seq'), may hold values from -256 to 256
- keys: bfloat16 [8, 12288, 1536], P('dp', 'seq'), may hold values from -6 to 6
- values: bfloat16 [8, 12288, 1536], P('dp', 'seq'), may hold values from -6 to 6
- cotangent: bfloat16 [8, 12288, 3072], P('dp', 'seq'), may hold values from -0.119628906 to 0.119628906
- adapter_down_weight: bfloat16 [1536, 64], replicated, may hold values from -0.15625 to 0.15625
- adapter_up_weight: bfloat16 [64, 3072], replicated, may hold values from -0.75 to 0.75
- tile_per_slot_block: int32 [8, 32], P('dp'), may hold values from 0 to 31, as said below
- tile_window_table: int32 [8, 32, 6], P('dp'), may hold values from -1 to 31, as said below
- real_token_count: int32 [8, 32], P('dp'), may hold values from 192 to 384
Outputs:
- attention: bfloat16 [8, 12288, 1536], P('dp', 'seq')
- grad_a: float32 [1536, 64], replicated
- grad_b: float32 [64, 3072], replicated
Inputs may be any that keep to these rules, and one draw needn't show every extreme that they name: `tile_per_slot_block`: tiles 2r and 2r+1 form pair r; slot blocks 2r and 2r+1 hold the two tiles of pair r, in either order. `tile_window_table`: tile t lies in frame-tile t // 8, tile row (t % 8) // 2 and column t % 2, and pair t // 2 is its row. Entry 0 of tile t's window is t, entry 1 the other tile of its pair; entries 2 to 5 are the two tiles of each of two other rows of the same frame-tile, within two rows of t's row, listed row by row, or -1 for a row that the window leaves out at an edge of the frame-tile.
All inputs are finite; a program needn't handle non-finite values.
Results may differ from a plain program's by a relative error of at most 0.013.
Values may be sent and summed in bfloat16 or wider, within the bound.
A program may use at most 128 MiB of HBM per device.

v0:
```python
import jax
import jax.numpy as jnp
from jax import lax
from jax.sharding import PartitionSpec as P

HEAD = 128


def from_behind(shard, axis, by):
    devices = lax.axis_size(axis)
    pairs = [(i, i + by) for i in range(devices) if 0 <= i + by < devices]
    return lax.ppermute(shard, axis, pairs)


def attend(query, key_rows, value_rows, key_mask):
    head_size = HEAD
    count = query.shape[1] // head_size
    scale = head_size ** (-0.5)

    def one_head(index):
        start = index * head_size
        qh = lax.dynamic_slice_in_dim(query, start, head_size, 1)
        kh = lax.dynamic_slice_in_dim(key_rows, start, head_size, 1)
        vh = lax.dynamic_slice_in_dim(value_rows, start, head_size, 1)
        scores = (
            lax.dot_general(qh, kh, (((1,), (1,)), ((), ())), preferred_element_type=jnp.float32)
            * scale
        )
        scores = jnp.where(key_mask[None, :], scores, jnp.float32(-1e30))
        top = jnp.max(scores, axis=1, keepdims=True)
        expo = jnp.exp(scores - top)
        total = jnp.sum(expo, axis=1, keepdims=True)
        weights = expo.astype(jnp.bfloat16)
        return jnp.dot(weights, vh, preferred_element_type=jnp.float32) / total

    heads_out = lax.map(one_head, jnp.arange(count, dtype=jnp.int32))
    return jnp.transpose(heads_out, (1, 0, 2)).reshape(query.shape[0], query.shape[1])


def per_device(
    queries,
    keys,
    values,
    cotangent,
    adapter_down_weight,
    adapter_up_weight,
    tile_per_slot_block,
    tile_window_table,
    real_token_count,
):
    here = lax.axis_index("seq")
    members = lax.axis_size("seq")
    tile_rows = queries.shape[1]
    width = queries.shape[2]
    order = tile_per_slot_block[0]
    valid = real_token_count[0]

    def tile_at(position):
        inside = (position >= 0) & (position < members)
        return jnp.where(inside, order[jnp.clip(position, 0, members - 1)], -1)

    mine = tile_at(here)
    window = lax.dynamic_index_in_dim(tile_window_table[0], mine, 0, keepdims=False)
    own_keys = keys[0]
    own_values = values[0]
    pieces_k = [own_keys]
    pieces_v = [own_values]
    tile_ids = [mine]
    for offset in (1, 2, 3, 4, 5, -1, -2, -3, -4, -5):
        moved = from_behind((own_keys, own_values), "seq", offset)
        pieces_k.append(moved[0])
        pieces_v.append(moved[1])
        tile_ids.append(tile_at(here - offset))
    stacked_k = jnp.stack(pieces_k)
    stacked_v = jnp.stack(pieces_v)
    ids = jnp.stack(tile_ids)
    places = jnp.arange(ids.shape[0], dtype=jnp.int32)
    present = window >= 0
    match = (ids[None, :] == window[:, None]) & present[:, None]
    index = jnp.sum(jnp.where(match, places[None, :], 0), axis=1)
    key_rows = jnp.take(stacked_k, index, axis=0).reshape(-1, width)
    value_rows = jnp.take(stacked_v, index, axis=0).reshape(-1, width)
    table = jnp.arange(valid.shape[0], dtype=jnp.int32)
    safe = jnp.where(present, window, 0)
    valid_of = jnp.sum(jnp.where(safe[:, None] == table[None, :], valid[None, :], 0), axis=1)
    slots = jnp.arange(tile_rows, dtype=jnp.int32)
    key_mask = (present[:, None] & (slots[None, :] < valid_of[:, None])).reshape(-1)
    own_valid = jnp.sum(jnp.where(table == mine, valid, 0))
    block_output = attend(queries[0], key_rows, value_rows, key_mask)
    block_output = jnp.where((slots < own_valid)[:, None], block_output, jnp.float32(0.0)).astype(
        jnp.bfloat16
    )
    incoming_gradients = cotangent[0]
    hidden_state = jnp.dot(
        block_output, adapter_down_weight, preferred_element_type=jnp.float32
    ).astype(jnp.bfloat16)
    backward_pass = lax.dot_general(
        incoming_gradients,
        adapter_up_weight,
        (((1,), (1,)), ((), ())),
        preferred_element_type=jnp.float32,
    ).astype(jnp.bfloat16)
    part_b = lax.dot_general(
        hidden_state,
        incoming_gradients,
        (((0,), (0,)), ((), ())),
        preferred_element_type=jnp.float32,
    )
    part_a = lax.dot_general(
        block_output, backward_pass, (((0,), (0,)), ((), ())), preferred_element_type=jnp.float32
    )
    grad_a, grad_b = lax.psum((part_a, part_b), ("seq", "dp"))
    return (block_output[None], grad_a, grad_b)


def solution(mesh):
    placed = (
        P("dp", "seq", None),
        P("dp", "seq", None),
        P("dp", "seq", None),
        P("dp", "seq", None),
        P(),
        P(),
        P("dp", None),
        P("dp", None, None),
        P("dp", None),
    )
    return jax.shard_map(
        per_device,
        mesh=mesh,
        in_specs=placed,
        out_specs=(P("dp", "seq", None), P(), P()),
        check_vma=False,
    )
```

profile of v0, /device:TPU:1, one launch (start us, length us, event | category | flops | bytes accessed | tf_op | source)
XLA Modules:
  0.0 835.7 jit_solution(6961464823817320602)
XLA Ops:
  7.2 5.2 collective-permute-start
  12.5 4.4 collective-permute-start.1
  16.9 4.4 collective-permute-start.2
  21.3 3.5 collective-permute-start.3
  24.8 3.6 collective-permute-start.4
  39.5 2.4 constant_dynamic-update-slice_fusion.1
  43.1 2.4 constant_dynamic-update-slice_fusion.2
  48.3 2.4 bitcast_dynamic-update-slice_fusion.19
  50.7 11.0 %collective-permute-done.1 = bf16[384,1536]{1,0:T(8,128)(2,1)} collective-permute-done((bf16[384,1536]{1,0:T(8,128)(2,1)}, bf16[384,1536]{1,0:T(8,128)(2,1)}, u32[]{:S(2)}, u32[]{:S(2)}) %collective-permute-start.1) | collective-permute-done | bytes 1179680 | tf_op jit(solution)/shard_map/ppermute | solution.py:12
  63.0 2.4 bitcast_dynamic-update-slice_fusion.18
  65.4 2.4 collective-permute-done.2
  69.0 2.4 bitcast_dynamic-update-slice_fusion.17
  72.7 2.4 bitcast_dynamic-update-slice_fusion.16
  76.4 2.4 bitcast_dynamic-update-slice_fusion.15
  78.8 35.9 %collective-permute-start.10 = (bf16[384,1536]{1,0:T(8,128)(2,1)}, bf16[384,1536]{1,0:T(8,128)(2,1)S(1)}, u32[]{:S(2)}, u32[]{:S(2)}) collective-permute-start(bf16[384,1536]{1,0:T(8,128)(2,1)} %bitcast.36), channel_id=1, source_target_pairs={{0,8},{8,16},{16,24},{24,32},{32,40},{40,48},{48,56},{56,64},{64,7... | collective-permute-start | bytes 3538952 | tf_op jit(solution)/shard_map/ppermute | solution.py:12
  115.8 77.1 %collective-permute-start.11 = (bf16[384,1536]{1,0:T(8,128)(2,1)}, bf16[384,1536]{1,0:T(8,128)(2,1)S(1)}, u32[]{:S(2)}, u32[]{:S(2)}) collective-permute-start(bf16[384,1536]{1,0:T(8,128)(2,1)} %bitcast.36), channel_id=1, source_target_pairs={{0,16},{8,24},{16,32},{24,40},{32,48},{40,56},{48,64},{56,72},{64,... | collective-permute-start | bytes 3538952 | tf_op jit(solution)/shard_map/ppermute | solution.py:12
  194.0 2.6 collective-permute-start.12
  197.7 28.8 %collective-permute-start.13 = (bf16[384,1536]{1,0:T(8,128)(2,1)}, bf16[384,1536]{1,0:T(8,128)(2,1)S(1)}, u32[]{:S(2)}, u32[]{:S(2)}) collective-permute-start(bf16[384,1536]{1,0:T(8,128)(2,1)} %bitcast.36), channel_id=1, source_target_pairs={{0,32},{8,40},{16,48},{24,56},{32,64},{40,72},{48,80},{56,88},{64,... | collective-permute-start | bytes 3538952 | tf_op jit(solution)/shard_map/ppermute | solution.py:12
  227.6 9.9 %collective-permute-start.14 = (bf16[384,1536]{1,0:T(8,128)(2,1)}, bf16[384,1536]{1,0:T(8,128)(2,1)S(1)}, u32[]{:S(2)}, u32[]{:S(2)}) collective-permute-start(bf16[384,1536]{1,0:T(8,128)(2,1)} %bitcast.36), channel_id=1, source_target_pairs={{0,40},{8,48},{16,56},{24,64},{32,72},{40,80},{48,88},{56,96},{64,... | collective-permute-start | bytes 3538952 | tf_op jit(solution)/shard_map/ppermute | solution.py:12
  243.5 70.8 %collective-permute-done.12 = bf16[384,1536]{1,0:T(8,128)(2,1)S(1)} collective-permute-done((bf16[384,1536]{1,0:T(8,128)(2,1)}, bf16[384,1536]{1,0:T(8,128)(2,1)S(1)}, u32[]{:S(2)}, u32[]{:S(2)}) %collective-permute-start.12) | collective-permute-done | bytes 1179680 | tf_op jit(solution)/shard_map/ppermute | solution.py:12
  323.8 9.0 %gather_fusion = bf16[6,384,1536]{2,1,0:T(8,128)(2,1)} fusion(bf16[11,384,1536]{2,1,0:T(8,128)(2,1)} %bitcast_dynamic-update-slice_fusion.10, s32[1024]{0:T(1024)S(1)} %pad_clamp_fusion), kind=kCustom, calls=%fused_computation.clone | custom fusion | bytes 14155800 | tf_op jit(solution)/shard_map/jit(_take)/gather | solution.py:81
  332.8 12.9 %collective-permute-done.17 = bf16[384,1536]{1,0:T(8,128)(2,1)S(1)} collective-permute-done((bf16[384,1536]{1,0:T(8,128)(2,1)}, bf16[384,1536]{1,0:T(8,128)(2,1)S(1)}, u32[]{:S(2)}, u32[]{:S(2)}) %collective-permute-start.17) | collective-permute-done | bytes 1179680 | tf_op jit(solution)/shard_map/ppermute | solution.py:12
  346.8 73.2 %collective-permute-done.18 = bf16[384,1536]{1,0:T(8,128)(2,1)} collective-permute-done((bf16[384,1536]{1,0:T(8,128)(2,1)}, bf16[384,1536]{1,0:T(8,128)(2,1)}, u32[]{:S(2)}, u32[]{:S(2)}) %collective-permute-start.18) | collective-permute-done | bytes 1179680 | tf_op jit(solution)/shard_map/ppermute | solution.py:12
  420.0 2.4 bitcast_dynamic-update-slice_fusion.1
  422.4 2.4 bitcast_dynamic-update-slice_fusion
  424.8 9.0 %gather_fusion.1 = bf16[6,384,1536]{2,1,0:T(8,128)(2,1)} fusion(bf16[11,384,1536]{2,1,0:T(8,128)(2,1)} %bitcast_dynamic-update-slice_fusion, s32[1024]{0:T(1024)S(1)} %pad_clamp_fusion), kind=kCustom, calls=%fused_computation.1.clone | custom fusion | bytes 14155800 | tf_op jit(solution)/shard_map/jit(_take)/gather | solution.py:82
  433.8 10.3 %broadcast_select_fusion = (bf16[6,384,1536]{2,1,0:T(8,128)(2,1)}, bf16[6,384,1536]{2,1,0:T(8,128)(2,1)}) fusion(bf16[6,384,1536]{2,1,0:T(8,128)(2,1)} %gather_fusion.1, pred[6]{0:T(512)(128)(4,1)S(1)} %copy-done.2, bf16[6,384,1536]{2,1,0:T(8,128)(2,1)} %gather_fusion), kind=kLoop, calls=%fused_computation.20 | loop fusion | flops 7077888 | bytes 28311558 | tf_op jit(solution)/shard_map/jit(_take)/select_n | solution.py:82
  444.1 77.0 %while.11 = (s32[]{:T(128)}, bf16[12,384,128]{1,2,0:T(8,128)(2,1)}, s32[12]{0:T(128)S(1)}, bf16[384,1536]{1,0:T(8,128)(2,1)}, bf16[2304,1536]{1,0:T(8,128)(2,1)}...) while((s32[]{:T(128)}, bf16[12,384,128]{1,2,0:T(8,128)(2,1)}, ...), condition=%wide.region_6.8_spmd.clone, body=%wide.region_3.7_spmd.clone.sunk | while | flops 459280128 | bytes 12404945 | solution.py:36
  522.6 2.7 fusion.22
  525.3 3.3 fusion.30
  531.6 293.4 %all-reduce.3.cloned.1.call-done = (f32[1536,64]{0,1:T(8,128)}, f32[64,3072]{1,0:T(8,128)}) async-done(((f32[1536,64]{0,1:T(8,128)}, f32[64,3072]{1,0:T(8,128)}), (f32[1536,64]{0,1:T(8,128)}, f32[64,3072]{1,0:T(8,128)})) %all-reduce.3.cloned.1.call-update) | async-done | bytes 1179664 | tf_op jit(solution)/shard_map/psum | solution.py:112
  826.8 2.1 copy.51
  (160 shorter events, 109.6 us)
Async XLA Ops:
  7.2 515.4 %copy-start = (bf16[1,384,3072]{2,1,0:T(8,128)(2,1)S(1)}, bf16[1,384,3072]{2,1,0:T(8,128)(2,1)}, u32[]{:S(2)}) copy-start(bf16[1,384,3072]{2,1,0:T(8,128)(2,1)} %param.16) | copy-start | bytes 7077892
  7.2 39.9 %copy-start.1 = (bf16[1,384,1536]{2,1,0:T(8,128)(2,1)S(1)}, bf16[1,384,1536]{2,1,0:T(8,128)(2,1)}, u32[]{:S(2)}) copy-start(bf16[1,384,1536]{2,1,0:T(8,128)(2,1)} %param.14) | copy-start | bytes 3538948
  7.2 817.8 %all-reduce.3.cloned.1.call-start = ((), (), s32[]{:S(2)}) async-start(), calls=%async_computation | async-start | bytes 2359296 | tf_op jit(solution)/shard_map/psum | solution.py:112
  7.2 39.8 %collective-permute-start = (bf16[384,1536]{1,0:T(8,128)(2,1)}, bf16[384,1536]{1,0:T(8,128)(2,1)}, u32[]{:S(2)}, u32[]{:S(2)}) collective-permute-start(bf16[384,1536]{1,0:T(8,128)(2,1)} %bitcast.104), channel_id=1, source_target_pairs={{0,8},{8,16},{16,24},{24,32},{32,40},{40,48},{48,56},{56,64},{64,7... | collective-permute-start | bytes 3538952 | tf_op jit(solution)/shard_map/ppermute | solution.py:12
  12.5 49.2 %collective-permute-start.1 = (bf16[384,1536]{1,0:T(8,128)(2,1)}, bf16[384,1536]{1,0:T(8,128)(2,1)}, u32[]{:S(2)}, u32[]{:S(2)}) collective-permute-start(bf16[384,1536]{1,0:T(8,128)(2,1)} %bitcast.105), channel_id=1, source_target_pairs={{0,16},{8,24},{16,32},{24,40},{32,48},{40,56},{48,64},{56,72},{64,... | collective-permute-start | bytes 3538952 | tf_op jit(solution)/shard_map/ppermute | solution.py:12
  16.9 50.8 %collective-permute-start.2 = (bf16[384,1536]{1,0:T(8,128)(2,1)}, bf16[384,1536]{1,0:T(8,128)(2,1)}, u32[]{:S(2)}, u32[]{:S(2)}) collective-permute-start(bf16[384,1536]{1,0:T(8,128)(2,1)} %bitcast.106), channel_id=1, source_target_pairs={{0,24},{8,32},{16,40},{24,48},{32,56},{40,64},{48,72},{56,80},{64,... | collective-permute-start | bytes 3538952 | tf_op jit(solution)/shard_map/ppermute | solution.py:12
  21.3 50.1 %collective-permute-start.3 = (bf16[384,1536]{1,0:T(8,128)(2,1)}, bf16[384,1536]{1,0:T(8,128)(2,1)}, u32[]{:S(2)}, u32[]{:S(2)}) collective-permute-start(bf16[384,1536]{1,0:T(8,128)(2,1)} %bitcast.107), channel_id=1, source_target_pairs={{0,32},{8,40},{16,48},{24,56},{32,64},{40,72},{48,80},{56,88},{64,... | collective-permute-start | bytes 3538952 | tf_op jit(solution)/shard_map/ppermute | solution.py:12
  24.8 50.3 %collective-permute-start.4 = (bf16[384,1536]{1,0:T(8,128)(2,1)}, bf16[384,1536]{1,0:T(8,128)(2,1)}, u32[]{:S(2)}, u32[]{:S(2)}) collective-permute-start(bf16[384,1536]{1,0:T(8,128)(2,1)} %bitcast.108), channel_id=1, source_target_pairs={{0,40},{8,48},{16,56},{24,64},{32,72},{40,80},{48,88},{56,96},{64,... | collective-permute-start | bytes 3538952 | tf_op jit(solution)/shard_map/ppermute | solution.py:12
  47.0 31.7 %collective-permute-start.5 = (bf16[384,1536]{1,0:T(8,128)(2,1)S(1)}, bf16[384,1536]{1,0:T(8,128)(2,1)S(1)}, u32[]{:S(2)}, u32[]{:S(2)}) collective-permute-start(bf16[384,1536]{1,0:T(8,128)(2,1)S(1)} %bitcast.109), channel_id=1, source_target_pairs={{8,0},{16,8},{24,16},{32,24},{40,32},{48,40},{56,48},{64,56},{72,6... | collective-permute-start | bytes 3538952 | tf_op jit(solution)/shard_map/ppermute | solution.py:12
  61.7 54.1 %collective-permute-start.6 = (bf16[384,1536]{1,0:T(8,128)(2,1)S(1)}, bf16[384,1536]{1,0:T(8,128)(2,1)S(1)}, u32[]{:S(2)}, u32[]{:S(2)}) collective-permute-start(bf16[384,1536]{1,0:T(8,128)(2,1)S(1)} %bitcast.110), channel_id=1, source_target_pairs={{16,0},{24,8},{32,16},{40,24},{48,32},{56,40},{64,48},{72,56},{80,... | collective-permute-start | bytes 3538952 | tf_op jit(solution)/shard_map/ppermute | solution.py:12
  67.8 126.3 %collective-permute-start.7 = (bf16[384,1536]{1,0:T(8,128)(2,1)S(1)}, bf16[384,1536]{1,0:T(8,128)(2,1)S(1)}, u32[]{:S(2)}, u32[]{:S(2)}) collective-permute-start(bf16[384,1536]{1,0:T(8,128)(2,1)S(1)} %bitcast.111), channel_id=1, source_target_pairs={{24,0},{32,8},{40,16},{48,24},{56,32},{64,40},{72,48},{80,56},{88,... | collective-permute-start | bytes 3538952 | tf_op jit(solution)/shard_map/ppermute | solution.py:12
  71.4 126.3 %collective-permute-start.8 = (bf16[384,1536]{1,0:T(8,128)(2,1)S(1)}, bf16[384,1536]{1,0:T(8,128)(2,1)S(1)}, u32[]{:S(2)}, u32[]{:S(2)}) collective-permute-start(bf16[384,1536]{1,0:T(8,128)(2,1)S(1)} %bitcast.112), channel_id=1, source_target_pairs={{32,0},{40,8},{48,16},{56,24},{64,32},{72,40},{80,48},{88,56},{96,... | collective-permute-start | bytes 3538952 | tf_op jit(solution)/shard_map/ppermute | solution.py:12
  75.1 152.5 %collective-permute-start.9 = (bf16[384,1536]{1,0:T(8,128)(2,1)S(1)}, bf16[384,1536]{1,0:T(8,128)(2,1)S(1)}, u32[]{:S(2)}, u32[]{:S(2)}) collective-permute-start(bf16[384,1536]{1,0:T(8,128)(2,1)S(1)} %bitcast.113), channel_id=1, source_target_pairs={{40,0},{48,8},{56,16},{64,24},{72,32},{80,40},{88,48},{96,56},{104... | collective-permute-start | bytes 3538952 | tf_op jit(solution)/shard_map/ppermute | solution.py:12
  78.8 159.9 %collective-permute-start.10 = (bf16[384,1536]{1,0:T(8,128)(2,1)}, bf16[384,1536]{1,0:T(8,128)(2,1)S(1)}, u32[]{:S(2)}, u32[]{:S(2)}) collective-permute-start(bf16[384,1536]{1,0:T(8,128)(2,1)} %bitcast.36), channel_id=1, source_target_pairs={{0,8},{8,16},{16,24},{24,32},{32,40},{40,48},{48,56},{56,64},{64,7... | collective-permute-start | bytes 3538952 | tf_op jit(solution)/shard_map/ppermute | solution.py:12
  115.8 125.3 %collective-permute-start.11 = (bf16[384,1536]{1,0:T(8,128)(2,1)}, bf16[384,1536]{1,0:T(8,128)(2,1)S(1)}, u32[]{:S(2)}, u32[]{:S(2)}) collective-permute-start(bf16[384,1536]{1,0:T(8,128)(2,1)} %bitcast.36), channel_id=1, source_target_pairs={{0,16},{8,24},{16,32},{24,40},{32,48},{40,56},{48,64},{56,72},{64,... | collective-permute-start | bytes 3538952 | tf_op jit(solution)/shard_map/ppermute | solution.py:12
  194.0 120.2 %collective-permute-start.12 = (bf16[384,1536]{1,0:T(8,128)(2,1)}, bf16[384,1536]{1,0:T(8,128)(2,1)S(1)}, u32[]{:S(2)}, u32[]{:S(2)}) collective-permute-start(bf16[384,1536]{1,0:T(8,128)(2,1)} %bitcast.36), channel_id=1, source_target_pairs={{0,24},{8,32},{16,40},{24,48},{32,56},{40,64},{48,72},{56,80},{64,... | collective-permute-start | bytes 3538952 | tf_op jit(solution)/shard_map/ppermute | solution.py:12
  197.7 118.9 %collective-permute-start.13 = (bf16[384,1536]{1,0:T(8,128)(2,1)}, bf16[384,1536]{1,0:T(8,128)(2,1)S(1)}, u32[]{:S(2)}, u32[]{:S(2)}) collective-permute-start(bf16[384,1536]{1,0:T(8,128)(2,1)} %bitcast.36), channel_id=1, source_target_pairs={{0,32},{8,40},{16,48},{24,56},{32,64},{40,72},{48,80},{56,88},{64,... | collective-permute-start | bytes 3538952 | tf_op jit(solution)/shard_map/ppermute | solution.py:12
  227.6 91.5 %collective-permute-start.14 = (bf16[384,1536]{1,0:T(8,128)(2,1)}, bf16[384,1536]{1,0:T(8,128)(2,1)S(1)}, u32[]{:S(2)}, u32[]{:S(2)}) collective-permute-start(bf16[384,1536]{1,0:T(8,128)(2,1)} %bitcast.36), channel_id=1, source_target_pairs={{0,40},{8,48},{16,56},{24,64},{32,72},{40,80},{48,88},{56,96},{64,... | collective-permute-start | bytes 3538952 | tf_op jit(solution)/shard_map/ppermute | solution.py:12
  238.7 82.8 %collective-permute-start.15 = (bf16[384,1536]{1,0:T(8,128)(2,1)}, bf16[384,1536]{1,0:T(8,128)(2,1)S(1)}, u32[]{:S(2)}, u32[]{:S(2)}) collective-permute-start(bf16[384,1536]{1,0:T(8,128)(2,1)} %bitcast.36), channel_id=1, source_target_pairs={{8,0},{16,8},{24,16},{32,24},{40,32},{48,40},{56,48},{64,56},{72,6... | collective-permute-start | bytes 3538952 | tf_op jit(solution)/shard_map/ppermute | solution.py:12
  241.1 81.6 %collective-permute-start.16 = (bf16[384,1536]{1,0:T(8,128)(2,1)}, bf16[384,1536]{1,0:T(8,128)(2,1)S(1)}, u32[]{:S(2)}, u32[]{:S(2)}) collective-permute-start(bf16[384,1536]{1,0:T(8,128)(2,1)} %bitcast.36), channel_id=1, source_target_pairs={{16,0},{24,8},{32,16},{40,24},{48,32},{56,40},{64,48},{72,56},{80,... | collective-permute-start | bytes 3538952 | tf_op jit(solution)/shard_map/ppermute | solution.py:12
  314.3 31.5 %collective-permute-start.17 = (bf16[384,1536]{1,0:T(8,128)(2,1)}, bf16[384,1536]{1,0:T(8,128)(2,1)S(1)}, u32[]{:S(2)}, u32[]{:S(2)}) collective-permute-start(bf16[384,1536]{1,0:T(8,128)(2,1)} %bitcast.36), channel_id=1, source_target_pairs={{24,0},{32,8},{40,16},{48,24},{56,32},{64,40},{72,48},{80,56},{88,... | collective-permute-start | bytes 3538952 | tf_op jit(solution)/shard_map/ppermute | solution.py:12
  316.7 103.4 %collective-permute-start.18 = (bf16[384,1536]{1,0:T(8,128)(2,1)}, bf16[384,1536]{1,0:T(8,128)(2,1)}, u32[]{:S(2)}, u32[]{:S(2)}) collective-permute-start(bf16[384,1536]{1,0:T(8,128)(2,1)} %bitcast.36), channel_id=1, source_target_pairs={{32,0},{40,8},{48,16},{56,24},{64,32},{72,40},{80,48},{88,56},{96,... | collective-permute-start | bytes 3538952 | tf_op jit(solution)/shard_map/ppermute | solution.py:12
  319.1 103.3 %collective-permute-start.19 = (bf16[384,1536]{1,0:T(8,128)(2,1)}, bf16[384,1536]{1,0:T(8,128)(2,1)}, u32[]{:S(2)}, u32[]{:S(2)}) collective-permute-start(bf16[384,1536]{1,0:T(8,128)(2,1)} %bitcast.36), channel_id=1, source_target_pairs={{40,0},{48,8},{56,16},{64,24},{72,32},{80,40},{88,48},{96,56},{104... | collective-permute-start | bytes 3538952 | tf_op jit(solution)/shard_map/ppermute | solution.py:12
  424.8 9.0 %copy-start.2 = (pred[6]{0:T(512)(128)(4,1)S(1)}, pred[6]{0:T(512)(128)(4,1)}, u32[]{:S(2)}) copy-start(pred[6]{0:T(512)(128)(4,1)} %compare_and_fusion) | copy-start | bytes 22
Sparse Core Ops, SparseCore 0:
  528.8 296.1 all-reduce.2
where the time goes:
time: 839 us; the launch traced here: 836 us
  waiting for transfers between devices  464 us (55%)
  starting transfers between devices  188 us (22%)
  local copies, waits for them, and re-layouts  78.7 us (9%)
  matrix products  50 us (6%)
  other arithmetic  25.8 us (3%)
  between operations  21.2 us (3%)
    psum x1, waiting for transfers between devices, per_device(): grad_a, grad_b = lax.psum((part_a, part_b), ('seq', 'dp'))  293 us
    ppermute x20, starting transfers between devices, from_behind(): return lax.ppermute(shard, axis, pairs)  188 us
    ppermute x20, waiting for transfers between devices, from_behind(): return lax.ppermute(shard, axis, pairs)  170 us
    unnamed x29, local copies, waits for them, and re-layouts  37.7 us
    dot_general x12, matrix products, one_head(): lax.dot_general(qh, kh, (((1,), (1,)), ((), ())), preferred_element_type=...  22.7 us
    dot_general x12, matrix products, one_head(): return jnp.dot(weights, vh, preferred_element_type=jnp.float32) / total  21.3 us
  transfers between devices with their start and end apart: 21, of which 6 were waited for; matrix products, arithmetic and copies ran while one was open for 6% of the time, Pallas kernels for 0%

commit v1 on v0

v1 whole, which is shorter than its diff:
```python
import functools
import math

import jax
import jax.numpy as jnp
from jax import lax
from jax.experimental import pallas as pl
from jax.experimental.pallas import tpu as pltpu
from jax.sharding import PartitionSpec as P

HEAD = 128
TILE = 384
WIN = 6
CHUNKS = 3
X, Z, Y = 4, 8, 4
SCALE = math.log2(math.e) / math.sqrt(HEAD)
NT = (((1,), (1,)), ((), ()))
TN = (((0,), (0,)), ((), ()))
MESH = pl.DeviceIdType.MESH
BF16, F32 = jnp.bfloat16, jnp.float32
VMEM_LIMIT = 58 * 2**20


def place():
    seq, dp = lax.axis_index("seq"), lax.axis_index("dp")
    return seq // X, seq % X, dp // 2, dp % 2


def device(z, x, y, core):
    return {"seq": z * X + x, "dp": y * 2 + core}


def columns(head):
    return pl.ds(pl.multiple_of(head * HEAD, HEAD), HEAD)


def attend_kernel(
    order, window, valid, q_in, k_in, v_in, cot_in, down, up,
    att_out, gb_out, ga_out,
    k_0, k_1, k_2, v_0, v_1, v_2, qbuf, obuf, att, cot, back, hidden,
    s_k, r_k, s_v, r_v, s_q, r_q, s_c, r_c, s_o, r_o, s_b, r_b, l_own, l_cot, l_att,
):
    kbuf, vbuf = (k_0, k_1, k_2), (v_0, v_1, v_2)
    z, x, y, core = place()
    plane = z % 2
    here = plane * X + x
    others = ((x + 2) % X, x + 1 - 2 * (x % 2), X - 1 - x)
    over_z = device(z + 1 - 2 * plane, x, y, core)

    def own(j, which):
        src = (k_in, v_in, q_in)[which].at[0, :, columns(X * j + x)]
        dst = (kbuf[j].at[here], vbuf[j].at[here], qbuf.at[j, x])[which]
        return pltpu.make_async_copy(src, dst, l_own.at[j, which])

    def spread(j, which, rel):
        there = others[rel]
        src = (k_in, v_in, q_in)[which].at[0, :, columns(X * j + there)]
        dst = (kbuf[j].at[here], vbuf[j].at[here], qbuf.at[j, x])[which]
        return pltpu.make_async_remote_copy(
            src_ref=src, dst_ref=dst,
            send_sem=(s_k, s_v, s_q)[which].at[j, rel],
            recv_sem=(r_k, r_v, r_q)[which].at[j, rel],
            device_id=device(z, there, y, core), device_id_type=MESH,
        )

    def across(j, which, rel):
        slot = plane * X + (others + (x,))[rel]
        ref = (kbuf, vbuf)[which][j].at[slot]
        return pltpu.make_async_remote_copy(
            src_ref=ref, dst_ref=ref,
            send_sem=s_c.at[j, which, rel], recv_sem=r_c.at[j, which, rel],
            device_id=over_z, device_id_type=MESH,
        )

    def result(j, rel, there):
        return pltpu.make_async_remote_copy(
            src_ref=obuf.at[j, rel], dst_ref=att.at[:, columns(X * j + x)],
            send_sem=s_o.at[j, rel], recv_sem=r_o.at[j, rel],
            device_id=device(z, there, y, core), device_id_type=MESH,
        )

    def share(rel):
        return pltpu.make_async_remote_copy(
            src_ref=back.at[x], dst_ref=back.at[x],
            send_sem=s_b.at[rel], recv_sem=r_b.at[rel],
            device_id=device(z, others[rel], y, core), device_id_type=MESH,
        )

    def write_out(j):
        part = pl.ds(X * HEAD * j, X * HEAD)
        return pltpu.make_async_copy(att.at[:, part], att_out.at[0, :, part], l_att.at[j])

    def issue(j, which):
        for rel in range(3):
            spread(j, which, rel).start()

    def forward(j):
        for rel in (1, 2, 0):
            for which in range(2):
                spread(j, which, rel).wait_recv()
                across(j, which, rel).start()

    def forward_own(j):
        for which in range(2):
            own(j, which).wait()
            across(j, which, 3).start()

    for j in range(CHUNKS):
        for which in range(3):
            own(j, which).start()
    cot_copy = pltpu.make_async_copy(cot_in.at[0], cot, l_cot)
    cot_copy.start()

    barrier = pltpu.get_barrier_semaphore()
    for there in others:
        pl.semaphore_signal(barrier, inc=1, device_id=device(z, there, y, core), device_id_type=MESH)
    pl.semaphore_signal(barrier, inc=1, device_id=over_z, device_id_type=MESH)
    pl.semaphore_wait(barrier, 4)

    issue(0, 0)
    issue(0, 1)
    forward_own(0)
    issue(1, 0)
    issue(1, 1)
    forward_own(1)
    issue(0, 2)
    forward(0)
    issue(2, 0)
    issue(2, 1)
    forward_own(2)
    issue(1, 2)
    issue(2, 2)
    cot_copy.wait()
    back[x] = lax.dot_general(up[...], cot[...], NT, preferred_element_type=F32).astype(BF16)
    for rel in range(3):
        share(rel).start()
    forward(1)

    def unit(j, step):
        there = jnp.where(step == 0, others[0], jnp.where(step == 1, others[1], jnp.where(step == 2, others[2], x)))
        tile = order[0, z * X + there]
        slots, biases = [], []
        lane = lax.broadcasted_iota(jnp.int32, (1, TILE), 1)
        for entry in range(WIN):
            wanted = window[0, tile, entry]
            present = wanted >= 0
            known = jnp.maximum(wanted, 0)
            first = known // 2 * 2
            slot = jnp.where(order[0, first] == known, first, first + 1) - (z // 2) * 2 * X
            slots.append(jnp.where(present, jnp.clip(slot, 0, 2 * X - 1), here))
            count = jnp.where(present, valid[0, known], 0)
            biases.append(jnp.where(lane < count, 0.0, -1e30).astype(F32))
        mine = valid[0, tile]
        half = TILE // 2
        for start in (0, half):
            query = qbuf[j, there, pl.ds(start, half), :]
            scores = []
            for entry in range(WIN):
                s = lax.dot_general(query, kbuf[j][slots[entry]], NT, preferred_element_type=F32)
                scores.append(s + biases[entry])
            top = functools.reduce(jnp.maximum, scores)
            top = jnp.max(top, axis=1, keepdims=True)
            total = None
            for entry in range(WIN):
                weights = jnp.exp2((scores[entry] - top) * SCALE).astype(BF16)
                value = vbuf[j][slots[entry]]
                value = jnp.concatenate([value, jnp.ones_like(value)], axis=1)
                part = jnp.dot(weights, value, preferred_element_type=F32)
                total = part if total is None else total + part
            row = start + lax.broadcasted_iota(jnp.int32, (half, HEAD), 0)
            out = jnp.where(row < mine, total[:, :HEAD] / total[:, HEAD:], 0.0)
            obuf[j, step, pl.ds(start, half), :] = out.astype(BF16)
        part_a = jnp.dot(back[there], obuf[j, step], preferred_element_type=F32)
        ga_out[:, j * HEAD:(j + 1) * HEAD] += part_a

        @pl.when(step < 3)
        def _():
            result(j, step, there).start()

        @pl.when(step == 3)
        def _():
            att[:, columns(X * j + x)] = obuf[j, 3]

    def collect(j):
        for rel in range(3):
            result(j, rel, others[rel]).wait_recv()
        write_out(j).start()
        part = slice(X * HEAD * j, X * HEAD * (j + 1))
        term = lax.dot_general(down[:, part], att[:, part], NT, preferred_element_type=F32)
        if j == 0:
            hidden[...] = term
        else:
            hidden[...] += term

    ga_out[...] = jnp.zeros_like(ga_out)
    for rel in range(3):
        share(rel).wait_recv()
    for j in range(CHUNKS):
        own(j, 2).wait()
        for rel in range(3):
            spread(j, 2, rel).wait_recv()
        for rel in range(4):
            for which in range(2):
                across(j, which, rel).wait_recv()

        def step_of(step, _, j=j):
            unit(j, step)
            if j == 0:
                @pl.when(step == 0)
                def _():
                    forward(2)
            return 0

        lax.fori_loop(0, X, step_of, 0)
        if j > 0:
            collect(j - 1)
    collect(CHUNKS - 1)
    gb_out[...] = jnp.dot(hidden[...].astype(BF16), cot[...], preferred_element_type=F32)
    for j in range(CHUNKS):
        write_out(j).wait()
        for rel in range(3):
            for which in range(3):
                spread(j, which, rel).wait_send()
            result(j, rel, others[rel]).wait_send()
        for rel in range(4):
            for which in range(2):
                across(j, which, rel).wait_send()
    for rel in range(3):
        share(rel).wait_send()


def attend(order, window, valid, queries, keys, values, cotangent, down, up):
    smem = pl.BlockSpec(memory_space=pltpu.SMEM)
    vmem = pl.BlockSpec(memory_space=pltpu.VMEM)
    hbm = pl.BlockSpec(memory_space=pl.ANY)
    dma = pltpu.SemaphoreType.DMA
    rank, wide = up.shape
    piece = (TILE, HEAD)
    return pl.pallas_call(
        attend_kernel,
        out_shape=(
            jax.ShapeDtypeStruct(queries.shape, BF16),
            jax.ShapeDtypeStruct((rank, wide), F32),
            jax.ShapeDtypeStruct((rank, CHUNKS * HEAD), F32),
        ),
        in_specs=[smem, smem, smem, hbm, hbm, hbm, hbm, vmem, vmem],
        out_specs=(hbm, vmem, vmem),
        scratch_shapes=[pltpu.VMEM((2 * X,) + piece, BF16)] * (2 * CHUNKS)
        + [
            pltpu.VMEM((CHUNKS, X) + piece, BF16),
            pltpu.VMEM((CHUNKS, X) + piece, BF16),
            pltpu.VMEM((TILE, CHUNKS * X * HEAD), BF16),
            pltpu.VMEM((TILE, wide), BF16),
            pltpu.VMEM((X, rank, TILE), BF16),
            pltpu.VMEM((rank, TILE), F32),
        ]
        + [dma((CHUNKS, 3))] * 6
        + [dma((CHUNKS, 2, 4))] * 2
        + [dma((CHUNKS, 3))] * 2
        + [dma((3,))] * 2
        + [dma((CHUNKS, 3)), dma, dma((CHUNKS,))],
        compiler_params=pltpu.CompilerParams(
            collective_id=0, has_side_effects=True, vmem_limit_bytes=VMEM_LIMIT
        ),
        name="attend",
    )(order, window, valid, queries, keys, values, cotangent, down, up)


def reduce_kernel(
    gb, ga, gb_out, ga_out,
    half_b, half_a, sent_b, sent_a, parts, parts_a, sums, final,
    s_0, r_0, s_1, r_1, s_a, r_a, s_2, r_2, s_3, r_3, s_4, r_4,
):
    z, x, y, core = place()
    rows = gb.shape[0] // 2
    band = rows // Y
    wide = gb.shape[1] // X
    across = device(z, x, y, 1 - core)
    square = [(dx, dy) for dx in range(X) for dy in range(Y) if (dx, dy) != (0, 0)]

    def at(dx, dy):
        return (x + dx) % X, (y + dy) % Y

    barrier = pltpu.get_barrier_semaphore()
    pl.semaphore_signal(barrier, inc=1, device_id=across, device_id_type=MESH)
    for dx, dy in square:
        tx, ty = at(dx, dy)
        pl.semaphore_signal(barrier, inc=1, device_id=device(z, tx, ty, core), device_id_type=MESH)
    for dz in range(1, Z):
        pl.semaphore_signal(barrier, inc=1, device_id=device((z + dz) % Z, x, y, core), device_id_type=MESH)
    pl.semaphore_wait(barrier, 1 + len(square) + Z - 1)

    def copy(src, dst, send, recv, to):
        return pltpu.make_async_remote_copy(
            src_ref=src, dst_ref=dst, send_sem=send, recv_sem=recv, device_id=to, device_id_type=MESH
        )

    keep = pl.ds(pl.multiple_of(core * rows, rows), rows)
    give = pl.ds(pl.multiple_of((1 - core) * rows, rows), rows)
    swaps = [
        copy(gb.at[give], half_b, s_0.at[0], r_0.at[0], across),
        copy(ga.at[give], half_a, s_0.at[1], r_0.at[1], across),
    ]
    for c in swaps:
        c.start()
    for c in swaps:
        c.wait()
    sent_b[...] = gb[keep, :] + half_b[...]
    sent_a[...] = ga[keep, :] + half_a[...]

    def band_of(ty):
        return pl.ds(pl.multiple_of(ty * band, band), band)

    def cols_of(tx):
        return pl.ds(pl.multiple_of(tx * wide, HEAD), wide)

    scatter = []
    for i, (dx, dy) in enumerate(square):
        tx, ty = at(dx, dy)
        to = device(z, tx, ty, core)
        scatter.append(
            copy(sent_b.at[band_of(ty), cols_of(tx)], parts.at[i], s_1.at[i], r_1.at[i], to)
        )
        if dx == 0:
            scatter.append(
                copy(sent_a.at[band_of(ty)], parts_a.at[dy - 1], s_a.at[dy - 1], r_a.at[dy - 1], to)
            )
    for c in scatter:
        c.start()
    for c in scatter:
        c.wait()
    piece_b = sent_b[band_of(y), cols_of(x)]
    for i in range(len(square)):
        piece_b += parts[i]
    piece_a = sent_a[band_of(y), :]
    for i in range(Y - 1):
        piece_a += parts_a[i]
    sums[z, :, :wide] = piece_b
    sums[z, :, wide:] = piece_a

    ring = [
        copy(sums.at[z], sums.at[z], s_2.at[dz - 1], r_2.at[dz - 1], device((z + dz) % Z, x, y, core))
        for dz in range(1, Z)
    ]
    for c in ring:
        c.start()
    for c in ring:
        c.wait()
    total = sums[0]
    for i in range(1, Z):
        total += sums[i]
    mine = pl.ds(pl.multiple_of(core * rows + y * band, band), band)
    final[x, mine, :] = total

    gather = [
        copy(final.at[x, mine], final.at[x, mine], s_3.at[i], r_3.at[i], device(z, *at(dx, dy), core))
        for i, (dx, dy) in enumerate(square)
    ]
    for c in gather:
        c.start()
    for c in gather:
        c.wait()
    last = copy(final.at[:, keep], final.at[:, keep], s_4.at[0], r_4.at[0], across)
    last.start()
    last.wait()
    for i in range(X):
        gb_out[:, i * wide:(i + 1) * wide] = final[i, :, :wide]
        for j in range(CHUNKS):
            head = X * j + i
            block = final[i, :, wide + j * HEAD:wide + (j + 1) * HEAD]
            ga_out[head * HEAD:(head + 1) * HEAD, :] = block.T


def reduce(gb, ga):
    vmem = pl.BlockSpec(memory_space=pltpu.VMEM)
    dma = pltpu.SemaphoreType.DMA
    rank, wide = gb.shape
    rows, band, part, part_a = rank // 2, rank // 2 // Y, wide // X, ga.shape[1]
    near = X * Y - 1
    return pl.pallas_call(
        reduce_kernel,
        out_shape=(
            jax.ShapeDtypeStruct((rank, wide), F32),
            jax.ShapeDtypeStruct((X * part_a, rank), F32),
        ),
        in_specs=[vmem, vmem],
        out_specs=(vmem, vmem),
        scratch_shapes=[
            pltpu.VMEM((rows, wide), F32),
            pltpu.VMEM((rows, part_a), F32),
            pltpu.VMEM((rows, wide), F32),
            pltpu.VMEM((rows, part_a), F32),
            pltpu.VMEM((near, band, part), F32),
            pltpu.VMEM((Y - 1, band, part_a), F32),
            pltpu.VMEM((Z, band, part + part_a), F32),
            pltpu.VMEM((X, rank, part + part_a), F32),
        ]
        + [dma((2,))] * 2
        + [dma((near,))] * 2
        + [dma((Y - 1,))] * 2
        + [dma((Z - 1,))] * 2
        + [dma((near,))] * 2
        + [dma((1,))] * 2,
        compiler_params=pltpu.CompilerParams(
            collective_id=1, has_side_effects=True, vmem_limit_bytes=VMEM_LIMIT
        ),
        name="reduce",
    )(gb, ga)


def per_device(queries, keys, values, cotangent, down, up, order, window, valid):
    attention, part_b, part_a = attend(
        order, window, valid, queries, keys, values, cotangent, down.T, up
    )
    grad_b, grad_a = reduce(part_b, part_a)
    return attention, grad_a, grad_b


def solution(mesh):
    placed = (
        P("dp", "seq", None),
        P("dp", "seq", None),
        P("dp", "seq", None),
        P("dp", "seq", None),
        P(),
        P(),
        P("dp", None),
        P("dp", None, None),
        P("dp", None),
    )
    return jax.shard_map(
        per_device,
        mesh=mesh,
        in_specs=placed,
        out_specs=(P("dp", "seq", None), P(), P()),
        check_vma=False,
    )
```

time: 839 us -> 124 us (0.15)
  waiting for transfers between devices: 464 us -> 0 us
  starting transfers between devices: 188 us -> 0 us
  Pallas kernels: 0 us -> 117 us
  local copies, waits for them, and re-layouts: 78.7 us -> 5.94 us
  matrix products: 50 us -> 0 us
  other arithmetic: 25.8 us -> 0 us
  between operations: 21.2 us -> 0.66 us
    psum x1 -> x0, waiting for transfers between devices: 293 us -> none  [per_device(): grad_a, grad_b = lax.psum((part_a, part_b), ('seq', 'dp'))]
    ppermute x20 -> x0, starting transfers between devices: 188 us -> none  [from_behind(): return lax.ppermute(shard, axis, pairs)]
    ppermute x20 -> x0, waiting for transfers between devices: 170 us -> none  [from_behind(): return lax.ppermute(shard, axis, pairs)]
    pallas_call x0 -> x2, Pallas kernels: none -> 117 us  [the longest x1 75.8 us: attend(): pl.pallas_call(attend_kernel, out_shape=(jax.ShapeDtypeStruct(queries.sha...]
    dot_general x26 -> x0, matrix products: 50 us -> none  [the longest x12 22.7 us: one_head(): lax.dot_general(qh, kh, (((1,), (1,)), ((), ())), preferred_element_type=...]
    unnamed x29 -> x8, local copies, waits for them, and re-layouts: 37.7 us -> 5.94 us
    gather x2 -> x0, local copies, waits for them, and re-layouts: 18 us -> none  [the longest x1 9.01 us: per_device(): key_rows = jnp.take(stacked_k, index, axis=0).reshape(-1, width)]
    select_n x3 -> x0, other arithmetic: 10.9 us -> none  [the longest x1 10.3 us: per_device(): value_rows = jnp.take(stacked_v, index, axis=0).reshape(-1, width)]
  transfers between devices with their start and end apart: 21 -> 0, of which waited for: 6 -> 0; matrix products, arithmetic and copies ran while one was open for 6% -> 0% of each run, Pallas kernels for 0% -> 0%
where the time goes in v1:
time: 124 us
  Pallas kernels  117 us (94%)
  local copies, waits for them, and re-layouts  5.94 us (5%)
    pallas_call x1, Pallas kernels, attend(): pl.pallas_call(attend_kernel, out_shape=(jax.ShapeDtypeStruct(queries.sha...  75.8 us
    pallas_call x1, Pallas kernels, reduce(): pl.pallas_call(reduce_kernel, out_shape=(jax.ShapeDtypeStruct((rank, wide...  41.3 us
    unnamed x8, local copies, waits for them, and re-layouts  5.94 us

profile of v1, /device:TPU:1, one launch (start us, length us, event | category | flops | bytes accessed | tf_op | source)
XLA Modules:
  0.0 123.7 jit_solution(6375569060992013885)
XLA Ops:
  0.6 1.4 %copy.12.window = s32[1,32,6]{2,1,0:T(8,128)} copy(s32[1,32,6]{1,0,2:T(1,128)} %param.16) | data formatting | bytes 1536 | tf_op args[7]
  2.0 75.8 %attend.1 = (bf16[1,384,1536]{2,1,0:T(8,128)(2,1)}, f32[64,3072]{1,0:T(8,128)}, f32[64,384]{1,0:T(8,128)}) custom-call(s32[1,32]{1,0:T(1,128)} %order.1, s32[1,32,6]{2,1,0:T(8,128)} %copy.12.window, s32[1,32]{1,0:T(1,128)} %valid.1, bf16[1,384,1536]{2,1,0:T(8,128)(2,1)} %q_in.1, bf16[1,384,1536]{2,1,0:T(8,128)(2,1)} %k_in.1, bf16[1,384,1536]{2,1,0:T(8,128)(2,1)} %v_in.1, ...), custom_call_target="tpu_custom_call" | custom-call | tf_op jit(solution)/shard_map/attend/pallas_call | solution.py:239
  77.8 0.0 copy-start
  77.8 41.3 %reduce.1 = (f32[64,3072]{1,0:T(8,128)}, f32[1536,64]{1,0:T(8,128)}) custom-call(f32[64,3072]{1,0:T(8,128)} %get-tuple-element.9.gb, f32[64,384]{1,0:T(8,128)} %get-tuple-element.10.ga), custom_call_target="tpu_custom_call" | custom-call | tf_op jit(solution)/shard_map/reduce/pallas_call | solution.py:380
  119.1 2.1 %copy.13 = f32[1536,64]{0,1:T(8,128)} copy(f32[1536,64]{1,0:T(8,128)} %get-tuple-element.14) | data formatting | bytes 786432
  121.2 0.0 copy-done
  121.2 0.0 copy-start.1
  121.3 1.0 copy.16
  122.3 0.5 copy-done.1
  122.8 0.9 copy.17
Async XLA Ops:
  77.8 43.5 %copy-start = (bf16[1,384,1536]{2,1,0:T(8,128)(2,1)S(1)}, bf16[1,384,1536]{2,1,0:T(8,128)(2,1)}, u32[]{:S(2)}) copy-start(bf16[1,384,1536]{2,1,0:T(8,128)(2,1)} %get-tuple-element.19) | copy-start | bytes 3538948
  121.2 1.6 %copy-start.1 = (f32[64,3072]{1,0:T(8,128)S(1)}, f32[64,3072]{1,0:T(8,128)}, u32[]{:S(2)}) copy-start(f32[64,3072]{1,0:T(8,128)} %get-tuple-element.21) | copy-start | bytes 2359300

commit v2 on v0

v2 whole, which is shorter than its diff:
```python
import functools
import math

import jax
import jax.numpy as jnp
from jax import lax
from jax.experimental import pallas as pl
from jax.experimental.pallas import tpu as pltpu
from jax.sharding import PartitionSpec as P

HEAD = 128
HEADS = 12
TILE = 384
WIN = 6
X, Z, Y = 4, 8, 4
GROUP = 2 * X
SCALE = math.log2(math.e) / math.sqrt(HEAD)
NT = (((1,), (1,)), ((), ()))
MESH = pl.DeviceIdType.MESH
BF16, F32 = jnp.bfloat16, jnp.float32
VMEM_LIMIT = 58 * 2**20
PART_B = 384
PART_A = 256
PART = PART_B + PART_A
SQUARE = [(dx, dy) for dx in range(X) for dy in range(Y) if (dx, dy) != (0, 0)]


def place():
    seq, dp = lax.axis_index("seq"), lax.axis_index("dp")
    return seq // X, seq % X, dp // 2, dp % 2


def device(z, x, y, core):
    return {"seq": z * X + x, "dp": y * 2 + core}


def columns(head):
    return pl.ds(pl.multiple_of(head * HEAD, HEAD), HEAD)


def remote(src, dst, send, recv, to):
    return pltpu.make_async_remote_copy(
        src_ref=src, dst_ref=dst, send_sem=send, recv_sem=recv, device_id=to, device_id_type=MESH
    )


def flip(a, b):
    return a + b - 2 * a * b


def kernel(
    order, window, valid, q_in, k_in, v_in, cot_in, down_t, up,
    att_out, sum_out,
    k_four, v_four, q_four, o_four, k_eight, v_eight, q_eight, o_eight,
    k_all, v_all, q_all, att, cot, back, hidden, grad_a,
    keep, give, got, acc, parts, sums, final,
    s_four, r_four, s_z, r_z, s_eight, r_eight, s_of, r_of, s_oe, r_oe,
    l_in, l_cot, l_att, l_sum,
    s_0, r_0, s_1, r_1, s_2, r_2, s_3, r_3, s_4, r_4,
):
    z, x, y, core = place()
    frame, plane = z // 2, z % 2
    here = plane * X + x
    staged = (k_all, v_all, q_all)
    fours = (k_four, v_four, q_four)
    eights = (k_eight, v_eight, q_eight)

    def slot_of(rel):
        return (
            4 * flip(plane, rel // 4) + 2 * flip(x // 2, rel // 2 % 2) + flip(x % 2, rel % 2)
        )

    def at_slot(slot):
        return device(2 * frame + slot // X, slot % X, y, core)

    over_core = device(z, x, y, 1 - core)

    def over_square(dx, dy):
        return device(z, (x + dx) % X, (y + dy) % Y, core)

    def over_ring(dz):
        return device((z + dz) % Z, x, y, core)

    def stage(part, which):
        width = X * HEAD
        span = pl.ds(part * width, width)
        return pltpu.make_async_copy(
            (k_in, v_in, q_in)[which].at[0, :, span], staged[which].at[:, span], l_in.at[part, which]
        )

    def four(which, rel):
        slot = slot_of(rel)
        dst = fours[which].at[here if which < 2 else x]
        return remote(
            staged[which].at[:, columns(slot % X)], dst,
            s_four.at[which, rel - 1], r_four.at[which, rel - 1], at_slot(slot),
        )

    def over_z(which, rel):
        ref = fours[which].at[slot_of(rel)]
        return remote(ref, ref, s_z.at[which, rel], r_z.at[which, rel], at_slot(slot_of(4)))

    def eight(which, rel):
        slot = slot_of(rel)
        return remote(
            staged[which].at[:, columns(X + slot)], eights[which].at[here],
            s_eight.at[which, rel - 1], r_eight.at[which, rel - 1], at_slot(slot),
        )

    def out_four(rel):
        slot = slot_of(rel)
        return remote(
            o_four.at[rel], att.at[:, columns(x)], s_of.at[rel - 1], r_of.at[rel - 1], at_slot(slot)
        )

    def out_eight(rel):
        slot = slot_of(rel)
        return remote(
            o_eight.at[rel], att.at[:, columns(X + here)], s_oe.at[rel - 1], r_oe.at[rel - 1],
            at_slot(slot),
        )

    def write_out(part):
        span = pl.ds(X * HEAD * part, X * HEAD * (part + 1))
        return pltpu.make_async_copy(att.at[:, span], att_out.at[0, :, span], l_att.at[part])

    for part in range(3):
        for which in range(3):
            stage(part, which).start()
    cot_copy = pltpu.make_async_copy(cot_in.at[0], cot, l_cot)
    cot_copy.start()

    partners = [at_slot(slot_of(rel)) for rel in range(1, GROUP)] + [over_core]
    partners += [over_square(dx, dy) for dx, dy in SQUARE if dy != 0]
    barrier = pltpu.get_barrier_semaphore()
    for to in partners:
        pl.semaphore_signal(barrier, inc=1, device_id=to, device_id_type=MESH)
    for dz in range(1, Z):
        @pl.when((z + dz) % Z != 2 * frame + 1 - plane)
        def _(dz=dz):
            pl.semaphore_signal(barrier, inc=1, device_id=over_ring(dz), device_id_type=MESH)
    pl.semaphore_wait(barrier, len(partners) + Z - 2)

    for which in range(3):
        stage(0, which).wait()
    for which in range(2):
        fours[which][here] = staged[which][:, columns(x)]
        for rel in (2, 1, 3):
            four(which, rel).start()
        over_z(which, 0).start()
    for rel in (2, 1, 3):
        four(2, rel).start()
    q_four[x] = q_all[:, columns(x)]
    for part in (1, 2):
        for which in range(3):
            stage(part, which).wait()
    for which in range(2):
        for rel in (2, 1, 3):
            eight(which, rel).start()
    for rel in (1, 3, 2):
        for which in range(2):
            four(which, rel).wait_recv()
            over_z(which, rel).start()
    for which in range(2):
        for rel in (4, 6, 5, 7):
            eight(which, rel).start()
    for rel in (2, 1, 3, 4, 6, 5, 7):
        eight(2, rel).start()
    for which in range(3):
        eights[which][here] = staged[which][:, columns(X + here)]
    cot_copy.wait()
    back[...] = lax.dot_general(up[...], cot[...], NT, preferred_element_type=F32).astype(BF16)
    grad_a[:, HEADS * HEAD:] = jnp.zeros((grad_a.shape[0], HEAD), F32)

    def unit(slot, query_of, key_of, value_of, out):
        tile = order[0, 2 * X * frame + slot]
        slots, biases = [], []
        lane = lax.broadcasted_iota(jnp.int32, (1, TILE), 1)
        for entry in range(WIN):
            wanted = window[entry, 0, tile]
            present = wanted >= 0
            known = jnp.maximum(wanted, 0)
            first = known // 2 * 2
            there = jnp.where(order[0, first] == known, first, first + 1) - frame * GROUP
            slots.append(jnp.where(present, jnp.clip(there, 0, GROUP - 1), here))
            count = jnp.where(present, valid[0, known], 0)
            biases.append(jnp.where(lane < count, 0.0, -1e30).astype(F32))
        mine = valid[0, tile]
        half = TILE // 2
        for start in (0, half):
            query = query_of[pl.ds(start, half), :]
            scores = []
            for entry in range(WIN):
                s = lax.dot_general(query, key_of[slots[entry]], NT, preferred_element_type=F32)
                scores.append(s + biases[entry])
            top = jnp.max(functools.reduce(jnp.maximum, scores), axis=1, keepdims=True)
            total = None
            for entry in range(WIN):
                weights = jnp.exp2((scores[entry] - top) * SCALE).astype(BF16)
                value = value_of[slots[entry]]
                value = jnp.concatenate([value, jnp.ones_like(value)], axis=1)
                term = jnp.dot(weights, value, preferred_element_type=F32)
                total = term if total is None else total + term
            row = start + lax.broadcasted_iota(jnp.int32, (half, HEAD), 0)
            result = jnp.where(row < mine, total[:, :HEAD] / total[:, HEAD:], 0.0)
            out[pl.ds(start, half), :] = result.astype(BF16)

    def collect(first, last):
        span = slice(first * HEAD, last * HEAD)
        term = lax.dot_general(down_t[:, span], att[:, span], NT, preferred_element_type=F32)
        hidden[...] = term if first == 0 else hidden[...] + term
        grad_a[:, span] = jnp.dot(back[...], att[:, span], preferred_element_type=F32)

    for rel in range(1, X):
        four(2, rel).wait_recv()
    for rel in range(X):
        for which in range(2):
            over_z(which, rel).wait_recv()

    def four_step(step, _):
        rel = (step + 1) % X
        slot = slot_of(rel)
        unit(slot, q_four.at[slot % X], k_four, v_four, o_four.at[rel])

        @pl.when(rel != 0)
        def _():
            out_four(rel).start()

        return 0

    lax.fori_loop(0, X, four_step, 0)
    att[:, columns(x)] = o_four[0]

    for which in range(2):
        for rel in range(1, GROUP):
            eight(which, rel).wait_recv()

    def eight_step(step, _):
        rel = (step + 1) % GROUP
        slot = slot_of(rel)

        @pl.when(rel != 0)
        def _():
            eight(2, rel).wait_recv()

        unit(slot, q_eight.at[slot], k_eight, v_eight, o_eight.at[rel])

        @pl.when(rel != 0)
        def _():
            out_eight(rel).start()

        @pl.when(step == 3)
        def _():
            for other in range(1, X):
                out_four(other).wait_recv()
            write_out(0).start()
            collect(0, X)

        return 0

    lax.fori_loop(0, GROUP, eight_step, 0)
    att[:, columns(X + here)] = o_eight[0]
    for rel in range(1, GROUP):
        out_eight(rel).wait_recv()
    write_out(1).start()
    collect(X, HEADS)

    mix = hidden[...].astype(BF16)

    def fill(ref, owner):
        for i in range(X):
            from_b = pl.ds(pl.multiple_of((2 * i + owner) * PART_B, HEAD), PART_B)
            from_a = pl.ds(pl.multiple_of(3 * HEAD * i + PART_A * owner, HEAD), PART_A)
            ref[:, i * PART:i * PART + PART_B] = jnp.dot(
                mix, cot[:, from_b], preferred_element_type=F32
            )
            ref[:, i * PART + PART_B:(i + 1) * PART] = grad_a[:, from_a]

    fill(give, 1 - core)
    swap = remote(give, got, s_0.at[0], r_0.at[0], over_core)
    swap.start()
    fill(keep, core)
    swap.wait()
    acc[...] = (keep[...] + got[...]).astype(BF16)

    band = acc.shape[0] // Y

    def rows_of(there):
        return pl.ds(pl.multiple_of(there * band, band), band)

    def piece_of(there):
        return pl.ds(pl.multiple_of(there * PART, HEAD), PART)

    scatter = [
        remote(
            acc.at[rows_of((y + dy) % Y), piece_of((x + dx) % X)], parts.at[i],
            s_1.at[i], r_1.at[i], over_square(dx, dy),
        )
        for i, (dx, dy) in enumerate(SQUARE)
    ]
    for c in scatter:
        c.start()
    for c in scatter:
        c.wait()
    piece = acc[rows_of(y), piece_of(x)].astype(F32)
    for i in range(len(SQUARE)):
        piece += parts[i].astype(F32)
    sums[z] = piece.astype(BF16)

    ring = [
        remote(sums.at[z], sums.at[z], s_2.at[dz - 1], r_2.at[dz - 1], over_ring(dz))
        for dz in range(1, Z)
    ]
    for c in ring:
        c.start()
    for c in ring:
        c.wait()
    total = sums[0].astype(F32)
    for i in range(1, Z):
        total += sums[i].astype(F32)
    final[core, x, rows_of(y), :] = total.astype(BF16)

    gather = [
        remote(
            final.at[core, x, rows_of(y)], final.at[core, x, rows_of(y)],
            s_3.at[i], r_3.at[i], over_square(dx, dy),
        )
        for i, (dx, dy) in enumerate(SQUARE)
    ]
    for c in gather:
        c.start()
    for c in gather:
        c.wait()
    last = remote(final.at[core], final.at[core], s_4.at[0], r_4.at[0], over_core)
    last.start()
    last.wait()
    save = pltpu.make_async_copy(final, sum_out, l_sum)
    save.start()

    for part in range(2):
        write_out(part).wait()
    for which in range(3):
        for rel in range(1, X):
            four(which, rel).wait_send()
        for rel in range(1, GROUP):
            eight(which, rel).wait_send()
    for which in range(2):
        for rel in range(X):
            over_z(which, rel).wait_send()
    for rel in range(1, X):
        out_four(rel).wait_send()
    for rel in range(1, GROUP):
        out_eight(rel).wait_send()
    save.wait()


def attend_and_sum(order, window, valid, queries, keys, values, cotangent, down, up):
    smem = pl.BlockSpec(memory_space=pltpu.SMEM)
    vmem = pl.BlockSpec(memory_space=pltpu.VMEM)
    hbm = pl.BlockSpec(memory_space=pl.ANY)
    dma = pltpu.SemaphoreType.DMA
    rank, wide = up.shape
    width = HEADS * HEAD
    near = len(SQUARE)

    def tiles(count):
        return pltpu.VMEM((count, TILE, HEAD), BF16)

    return pl.pallas_call(
        kernel,
        out_shape=(
            jax.ShapeDtypeStruct(queries.shape, BF16),
            jax.ShapeDtypeStruct((2, X, rank, PART), BF16),
        ),
        in_specs=[smem, smem, smem, hbm, hbm, hbm, hbm, vmem, vmem],
        out_specs=(hbm, hbm),
        scratch_shapes=[tiles(GROUP), tiles(GROUP), tiles(X), tiles(X)]
        + [tiles(GROUP)] * 4
        + [pltpu.VMEM((TILE, width), BF16)] * 4
        + [
            pltpu.VMEM((TILE, wide), BF16),
            pltpu.VMEM((rank, TILE), BF16),
            pltpu.VMEM((rank, TILE), F32),
            pltpu.VMEM((rank, width + HEAD), F32),
        ]
        + [pltpu.VMEM((rank, X * PART), F32)] * 3
        + [
            pltpu.VMEM((rank, X * PART), BF16),
            pltpu.VMEM((near, rank // Y, PART), BF16),
            pltpu.VMEM((Z, rank // Y, PART), BF16),
            pltpu.VMEM((2, X, rank, PART), BF16),
        ]
        + [dma((3, X - 1))] * 2
        + [dma((2, X))] * 2
        + [dma((3, GROUP - 1))] * 2
        + [dma((X - 1,))] * 2
        + [dma((GROUP - 1,))] * 2
        + [dma((3, 3)), dma, dma((2,)), dma]
        + [dma((1,))] * 2
        + [dma((near,))] * 2
        + [dma((Z - 1,))] * 2
        + [dma((near,))] * 2
        + [dma((1,))] * 2,
        compiler_params=pltpu.CompilerParams(
            collective_id=0, has_side_effects=True, vmem_limit_bytes=VMEM_LIMIT
        ),
        name="attend",
    )(order, window, valid, queries, keys, values, cotangent, down, up)


def finish_kernel(att_in, sum_in, att_out, gb_out, ga_out, held, sems):
    take = pltpu.make_async_copy(att_in, held, sems.at[0])
    put = pltpu.make_async_copy(held, att_out, sems.at[1])
    take.start()
    for i in range(X):
        for core in range(2):
            first = (2 * i + core) * PART_B
            gb_out[:, first:first + PART_B] = sum_in[core, i, :, :PART_B].astype(F32)
        for j in range(3):
            core, start = j // 2, PART_B + j % 2 * HEAD
            block = sum_in[core, i, :, start:start + HEAD].astype(F32)
            ga_out[:, (3 * i + j) * HEAD:(3 * i + j + 1) * HEAD] = block
        if i == 0:
            take.wait()
            put.start()
    put.wait()


def finish(attention, summed, wide):
    vmem = pl.BlockSpec(memory_space=pltpu.VMEM)
    hbm = pl.BlockSpec(memory_space=pl.ANY)
    rank = summed.shape[2]
    return pl.pallas_call(
        finish_kernel,
        out_shape=(
            jax.ShapeDtypeStruct(attention.shape, BF16),
            jax.ShapeDtypeStruct((rank, wide), F32),
            jax.ShapeDtypeStruct((rank, HEADS * HEAD), F32),
        ),
        in_specs=[hbm, vmem],
        out_specs=(hbm, vmem, vmem),
        scratch_shapes=[pltpu.VMEM(attention.shape, BF16), pltpu.SemaphoreType.DMA((2,))],
        compiler_params=pltpu.CompilerParams(vmem_limit_bytes=VMEM_LIMIT),
        name="finish",
    )(attention, summed)


def per_device(queries, keys, values, cotangent, down, up, order, window, valid):
    attention, summed = attend_and_sum(
        order, window.transpose(2, 0, 1), valid, queries, keys, values, cotangent, down.T, up
    )
    attention, grad_b, grad_a = finish(attention, summed, up.shape[1])
    return attention, grad_a.T, grad_b


def solution(mesh):
    placed = (
        P("dp", "seq", None),
        P("dp", "seq", None),
        P("dp", "seq", None),
        P("dp", "seq", None),
        P(),
        P(),
        P("dp", None),
        P("dp", None, None),
        P("dp", None),
    )
    return jax.shard_map(
        per_device,
        mesh=mesh,
        in_specs=placed,
        out_specs=(P("dp", "seq", None), P(), P()),
        check_vma=False,
    )
```

time: 839 us -> 103 us (0.12)
  waiting for transfers between devices: 464 us -> 0 us
  starting transfers between devices: 188 us -> 0 us
  Pallas kernels: 0 us -> 102 us
  local copies, waits for them, and re-layouts: 78.7 us -> 0 us
  matrix products: 50 us -> 0 us
  other arithmetic: 25.8 us -> 0 us
  between operations: 21.2 us -> 0.64 us
    psum x1 -> x0, waiting for transfers between devices: 293 us -> none  [per_device(): grad_a, grad_b = lax.psum((part_a, part_b), ('seq', 'dp'))]
    ppermute x20 -> x0, starting transfers between devices: 188 us -> none  [from_behind(): return lax.ppermute(shard, axis, pairs)]
    ppermute x20 -> x0, waiting for transfers between devices: 170 us -> none  [from_behind(): return lax.ppermute(shard, axis, pairs)]
    pallas_call x0 -> x2, Pallas kernels: none -> 102 us  [the longest x1 98 us: attend_and_sum(): pl.pallas_call(kernel, out_shape=(jax.ShapeDtypeStruct(queries.shape, BF1...]
    dot_general x26 -> x0, matrix products: 50 us -> none  [the longest x12 22.7 us: one_head(): lax.dot_general(qh, kh, (((1,), (1,)), ((), ())), preferred_element_type=...]
    unnamed x29 -> x0, local copies, waits for them, and re-layouts: 37.7 us -> none
    gather x2 -> x0, local copies, waits for them, and re-layouts: 18 us -> none  [the longest x1 9.01 us: per_device(): key_rows = jnp.take(stacked_k, index, axis=0).reshape(-1, width)]
    select_n x3 -> x0, other arithmetic: 10.9 us -> none  [the longest x1 10.3 us: per_device(): value_rows = jnp.take(stacked_v, index, axis=0).reshape(-1, width)]
  transfers between devices with their start and end apart: 21 -> 0, of which waited for: 6 -> 0; matrix products, arithmetic and copies ran while one was open for 6% -> 0% of each run, Pallas kernels for 0% -> 0%
where the time goes in v2:
time: 103 us
  Pallas kernels  102 us (99%)
    pallas_call x1, Pallas kernels, attend_and_sum(): pl.pallas_call(kernel, out_shape=(jax.ShapeDtypeStruct(queries.shape, BF1...  98 us
    pallas_call x1, Pallas kernels, finish(): pl.pallas_call(finish_kernel, out_shape=(jax.ShapeDtypeStruct(attention.s...  4.39 us

profile of v2, /device:TPU:1, one launch (start us, length us, event | category | flops | bytes accessed | tf_op | source)
XLA Modules:
  0.0 103.0 jit_solution(5471971776819617668)
XLA Ops:
  0.6 98.0 %attend.1 = (bf16[1,384,1536]{2,1,0:T(8,128)(2,1)}, bf16[2,4,64,640]{3,2,1,0:T(8,128)(2,1)}) custom-call(s32[1,32]{1,0:T(1,128)} %order.1, s32[6,1,32]{2,1,0:T(1,128)} %bitcast.4, s32[1,32]{1,0:T(1,128)} %valid.1, bf16[1,384,1536]{2,1,0:T(8,128)(2,1)} %q_in.1, bf16[1,384,1536]{2,1,0:T(8,128)(2,1)} %k_in.1, bf16[1,384,1536]{2,1,0:T(8,128)(2,1)} %v_in.1, ...), custom_call_target="tpu_custom_call" | custom-call | tf_op jit(solution)/shard_map/attend/pallas_call | solution.py:369
  98.6 4.4 %finish.1 = (bf16[1,384,1536]{2,1,0:T(8,128)(2,1)}, f32[64,3072]{1,0:T(8,128)}, f32[64,1536]{1,0:T(8,128)}) custom-call(bf16[1,384,1536]{2,1,0:T(8,128)(2,1)} %get-tuple-element.8.att_in, bf16[2,4,64,640]{3,2,1,0:T(8,128)(2,1)} %get-tuple-element.9.sum_in), custom_call_target="tpu_custom_call" | custom-call | tf_op jit(solution)/shard_map/finish/pallas_call | solution.py:433

commit v3 on v2

--- a/solution.py
+++ b/solution.py
@@ -22,7 +22,8 @@
 PART_B = 384
 PART_A = 256
 PART = PART_B + PART_A
-SQUARE = [(dx, dy) for dx in range(X) for dy in range(Y) if (dx, dy) != (0, 0)]
+FAR_FIRST = (2, 1, 3, 0)
+SQUARE = [(dx, dy) for dx in FAR_FIRST for dy in (2, 1, 3, 0) if (dx, dy) != (0, 0)]
 
 
 def place():
@@ -49,13 +50,14 @@
 
 
 def kernel(
-    order, window, valid, q_in, k_in, v_in, cot_in, down_t, up,
+    order_in, window_in, valid_in, q_in, k_in, v_in, cot_in, down_in, up_in,
     att_out, sum_out,
+    order, window, valid, down_t, up,
     k_four, v_four, q_four, o_four, k_eight, v_eight, q_eight, o_eight,
     k_all, v_all, q_all, att, cot, back, hidden, grad_a,
     keep, give, got, acc, parts, sums, final,
     s_four, r_four, s_z, r_z, s_eight, r_eight, s_of, r_of, s_oe, r_oe,
-    l_in, l_cot, l_att, l_sum,
+    l_in, l_small, l_att, l_sum,
     s_0, r_0, s_1, r_1, s_2, r_2, s_3, r_3, s_4, r_4,
 ):
     z, x, y, core = place()
@@ -75,9 +77,6 @@
 
     over_core = device(z, x, y, 1 - core)
 
-    def over_square(dx, dy):
-        return device(z, (x + dx) % X, (y + dy) % Y, core)
-
     def over_ring(dz):
         return device((z + dz) % Z, x, y, core)
 
@@ -124,14 +123,8 @@
         span = pl.ds(X * HEAD * part, X * HEAD * (part + 1))
         return pltpu.make_async_copy(att.at[:, span], att_out.at[0, :, span], l_att.at[part])
 
-    for part in range(3):
-        for which in range(3):
-            stage(part, which).start()
-    cot_copy = pltpu.make_async_copy(cot_in.at[0], cot, l_cot)
-    cot_copy.start()
-
     partners = [at_slot(slot_of(rel)) for rel in range(1, GROUP)] + [over_core]
-    partners += [over_square(dx, dy) for dx, dy in SQUARE if dy != 0]
+    partners += [device(z, (x + dx) % X, (y + dy) % Y, core) for dx, dy in SQUARE if dy != 0]
     barrier = pltpu.get_barrier_semaphore()
     for to in partners:
         pl.semaphore_signal(barrier, inc=1, device_id=to, device_id_type=MESH)
@@ -139,6 +132,20 @@
         @pl.when((z + dz) % Z != 2 * frame + 1 - plane)
         def _(dz=dz):
             pl.semaphore_signal(barrier, inc=1, device_id=over_ring(dz), device_id_type=MESH)
+    small = [
+        pltpu.make_async_copy(src, dst, l_small.at[i])
+        for i, (src, dst) in enumerate(
+            (
+                (up_in, up), (down_in, down_t), (order_in, order), (window_in, window),
+                (valid_in, valid), (cot_in.at[0], cot),
+            )
+        )
+    ]
+    for part in range(3):
+        for which in range(3):
+            stage(part, which).start()
+    for move in small:
+        move.start()
     pl.semaphore_wait(barrier, len(partners) + Z - 2)
 
     for which in range(3):
@@ -147,28 +154,33 @@
         fours[which][here] = staged[which][:, columns(x)]
         for rel in (2, 1, 3):
             four(which, rel).start()
-        over_z(which, 0).start()
-    for rel in (2, 1, 3):
-        four(2, rel).start()
-    q_four[x] = q_all[:, columns(x)]
+            if rel == 2:
+                over_z(which, 0).start()
     for part in (1, 2):
         for which in range(3):
             stage(part, which).wait()
-    for which in range(2):
-        for rel in (2, 1, 3):
-            eight(which, rel).start()
+    for which in range(3):
+        eight(which, 4).start()
+    q_four[x] = q_all[:, columns(x)]
+    along = [four(2, rel) for rel in (2, 1, 3)]
+    along += [eight(which, rel) for which in range(2) for rel in (2, 1, 3)]
     for rel in (1, 3, 2):
         for which in range(2):
             four(which, rel).wait_recv()
             over_z(which, rel).start()
-    for which in range(2):
-        for rel in (4, 6, 5, 7):
+            for c in along[:2 - which]:
+                c.start()
+            along = along[2 - which:]
+    for other, rel in ((2, 6), (1, 5), (3, 7)):
+        for which in range(2):
             eight(which, rel).start()
-    for rel in (2, 1, 3, 4, 6, 5, 7):
+        eight(2, other).start()
+    for rel in (6, 5, 7):
         eight(2, rel).start()
     for which in range(3):
         eights[which][here] = staged[which][:, columns(X + here)]
-    cot_copy.wait()
+    for move in small:
+        move.wait()
     back[...] = lax.dot_general(up[...], cot[...], NT, preferred_element_type=F32).astype(BF16)
     grad_a[:, HEADS * HEAD:] = jnp.zeros((grad_a.shape[0], HEAD), F32)
 
@@ -267,43 +279,44 @@
 
     mix = hidden[...].astype(BF16)
 
-    def fill(ref, owner):
-        for i in range(X):
-            from_b = pl.ds(pl.multiple_of((2 * i + owner) * PART_B, HEAD), PART_B)
-            from_a = pl.ds(pl.multiple_of(3 * HEAD * i + PART_A * owner, HEAD), PART_A)
-            ref[:, i * PART:i * PART + PART_B] = jnp.dot(
-                mix, cot[:, from_b], preferred_element_type=F32
-            )
-            ref[:, i * PART + PART_B:(i + 1) * PART] = grad_a[:, from_a]
-
-    fill(give, 1 - core)
-    swap = remote(give, got, s_0.at[0], r_0.at[0], over_core)
-    swap.start()
-    fill(keep, core)
-    swap.wait()
-    acc[...] = (keep[...] + got[...]).astype(BF16)
-
-    band = acc.shape[0] // Y
+    band = acc.shape[1] // Y
 
     def rows_of(there):
         return pl.ds(pl.multiple_of(there * band, band), band)
 
-    def piece_of(there):
-        return pl.ds(pl.multiple_of(there * PART, HEAD), PART)
+    def over_square(dx, dy):
+        return device(z, (x + dx) % X, (y + dy) % Y, core)
+
+    def fill(ref, dx, owner):
+        i = (x + dx) % X
+        from_b = pl.ds(pl.multiple_of((2 * i + owner) * PART_B, HEAD), PART_B)
+        from_a = pl.ds(pl.multiple_of(3 * HEAD * i + PART_A * owner, HEAD), PART_A)
+        ref[dx, :, :PART_B] = jnp.dot(mix, cot[:, from_b], preferred_element_type=F32)
+        ref[dx, :, PART_B:] = grad_a[:, from_a]
+
+    def swap(dx):
+        return remote(give.at[dx], got.at[dx], s_0.at[dx], r_0.at[dx], over_core)
 
     scatter = [
         remote(
-            acc.at[rows_of((y + dy) % Y), piece_of((x + dx) % X)], parts.at[i],
-            s_1.at[i], r_1.at[i], over_square(dx, dy),
+            acc.at[dx, rows_of((y + dy) % Y)], parts.at[i], s_1.at[i], r_1.at[i],
+            over_square(dx, dy),
         )
         for i, (dx, dy) in enumerate(SQUARE)
     ]
-    for c in scatter:
-        c.start()
-    for c in scatter:
-        c.wait()
-    piece = acc[rows_of(y), piece_of(x)].astype(F32)
+    for dx in FAR_FIRST:
+        fill(give, dx, 1 - core)
+        swap(dx).start()
+    for dx in FAR_FIRST:
+        fill(keep, dx, core)
+        swap(dx).wait_recv()
+        acc[dx] = (keep[dx] + got[dx]).astype(BF16)
+        for c, (to, _) in zip(scatter, SQUARE):
+            if to == dx:
+                c.start()
+    piece = acc[0, rows_of(y)].astype(F32)
     for i in range(len(SQUARE)):
+        scatter[i].wait_recv()
         piece += parts[i].astype(F32)
     sums[z] = piece.astype(BF16)
 
@@ -330,10 +343,10 @@
     for c in gather:
         c.start()
     for c in gather:
-        c.wait()
+        c.wait_recv()
     last = remote(final.at[core], final.at[core], s_4.at[0], r_4.at[0], over_core)
     last.start()
-    last.wait()
+    last.wait_recv()
     save = pltpu.make_async_copy(final, sum_out, l_sum)
     save.start()
 
@@ -351,12 +364,14 @@
         out_four(rel).wait_send()
     for rel in range(1, GROUP):
         out_eight(rel).wait_send()
+    for dx in range(X):
+        swap(dx).wait_send()
+    for c in scatter + gather + [last]:
+        c.wait_send()
     save.wait()
 
 
 def attend_and_sum(order, window, valid, queries, keys, values, cotangent, down, up):
-    smem = pl.BlockSpec(memory_space=pltpu.SMEM)
-    vmem = pl.BlockSpec(memory_space=pltpu.VMEM)
     hbm = pl.BlockSpec(memory_space=pl.ANY)
     dma = pltpu.SemaphoreType.DMA
     rank, wide = up.shape
@@ -372,9 +387,11 @@
             jax.ShapeDtypeStruct(queries.shape, BF16),
             jax.ShapeDtypeStruct((2, X, rank, PART), BF16),
         ),
-        in_specs=[smem, smem, smem, hbm, hbm, hbm, hbm, vmem, vmem],
+        in_specs=[hbm] * 9,
         out_specs=(hbm, hbm),
-        scratch_shapes=[tiles(GROUP), tiles(GROUP), tiles(X), tiles(X)]
+        scratch_shapes=[pltpu.SMEM(t.shape, t.dtype) for t in (order, window, valid)]
+        + [pltpu.VMEM(down.shape, BF16), pltpu.VMEM(up.shape, BF16)]
+        + [tiles(GROUP), tiles(GROUP), tiles(X), tiles(X)]
         + [tiles(GROUP)] * 4
         + [pltpu.VMEM((TILE, width), BF16)] * 4
         + [
@@ -383,9 +400,9 @@
             pltpu.VMEM((rank, TILE), F32),
             pltpu.VMEM((rank, width + HEAD), F32),
         ]
-        + [pltpu.VMEM((rank, X * PART), F32)] * 3
+        + [pltpu.VMEM((X, rank, PART), F32)] * 3
         + [
-            pltpu.VMEM((rank, X * PART), BF16),
+            pltpu.VMEM((X, rank, PART), BF16),
             pltpu.VMEM((near, rank // Y, PART), BF16),
             pltpu.VMEM((Z, rank // Y, PART), BF16),
             pltpu.VMEM((2, X, rank, PART), BF16),
@@ -395,8 +412,8 @@
         + [dma((3, GROUP - 1))] * 2
         + [dma((X - 1,))] * 2
         + [dma((GROUP - 1,))] * 2
-        + [dma((3, 3)), dma, dma((2,)), dma]
-        + [dma((1,))] * 2
+        + [dma((3, 3)), dma((6,)), dma((2,)), dma]
+        + [dma((X,))] * 2
         + [dma((near,))] * 2
         + [dma((Z - 1,))] * 2
         + [dma((near,))] * 2
@@ -408,38 +425,43 @@
     )(order, window, valid, queries, keys, values, cotangent, down, up)
 
 
-def finish_kernel(att_in, sum_in, att_out, gb_out, ga_out, held, sems):
-    take = pltpu.make_async_copy(att_in, held, sems.at[0])
-    put = pltpu.make_async_copy(held, att_out, sems.at[1])
-    take.start()
+def finish_kernel(att_in, sum_in, att_out, gb_out, ga_out, att, summed, gb, ga, sems):
+    take_sum = pltpu.make_async_copy(sum_in, summed, sems.at[0])
+    take_att = pltpu.make_async_copy(att_in, att, sems.at[1])
+    put_att = pltpu.make_async_copy(att, att_out, sems.at[2])
+    put_gb = pltpu.make_async_copy(gb, gb_out, sems.at[3])
+    put_ga = pltpu.make_async_copy(ga, ga_out, sems.at[4])
+    take_sum.start()
+    take_att.start()
+    take_sum.wait()
     for i in range(X):
         for core in range(2):
             first = (2 * i + core) * PART_B
-            gb_out[:, first:first + PART_B] = sum_in[core, i, :, :PART_B].astype(F32)
-        for j in range(3):
-            core, start = j // 2, PART_B + j % 2 * HEAD
-            block = sum_in[core, i, :, start:start + HEAD].astype(F32)
-            ga_out[:, (3 * i + j) * HEAD:(3 * i + j + 1) * HEAD] = block
-        if i == 0:
-            take.wait()
-            put.start()
-    put.wait()
+            gb[:, first:first + PART_B] = summed[core, i, :, :PART_B].astype(F32)
+    put_gb.start()
+    for head in range(HEADS):
+        i, j = head // 3, head % 3
+        start = PART_B + j % 2 * HEAD
+        ga[:, head * HEAD:(head + 1) * HEAD] = summed[j // 2, i, :, start:start + HEAD].astype(F32)
+    put_ga.start()
+    take_att.wait()
+    put_att.start()
+    put_gb.wait()
+    put_ga.wait()
+    put_att.wait()
 
 
 def finish(attention, summed, wide):
-    vmem = pl.BlockSpec(memory_space=pltpu.VMEM)
     hbm = pl.BlockSpec(memory_space=pl.ANY)
     rank = summed.shape[2]
+    shapes = ((attention.shape, BF16), ((rank, wide), F32), ((rank, HEADS * HEAD), F32))
+    held = (shapes[0], (summed.shape, BF16), shapes[1], shapes[2])
     return pl.pallas_call(
         finish_kernel,
-        out_shape=(
-            jax.ShapeDtypeStruct(attention.shape, BF16),
-            jax.ShapeDtypeStruct((rank, wide), F32),
-            jax.ShapeDtypeStruct((rank, HEADS * HEAD), F32),
-        ),
-        in_specs=[hbm, vmem],
-        out_specs=(hbm, vmem, vmem),
-        scratch_shapes=[pltpu.VMEM(attention.shape, BF16), pltpu.SemaphoreType.DMA((2,))],
+        out_shape=tuple(jax.ShapeDtypeStruct(*each) for each in shapes),
+        in_specs=[hbm, hbm],
+        out_specs=(hbm, hbm, hbm),
+        scratch_shapes=[pltpu.VMEM(*each) for each in held] + [pltpu.SemaphoreType.DMA((5,))],
         compiler_params=pltpu.CompilerParams(vmem_limit_bytes=VMEM_LIMIT),
         name="finish",
     )(attention, summed)

time: 103 us -> 96.2 us (0.934)
  Pallas kernels: 102 us -> 95.4 us
    pallas_call x1, Pallas kernels: 98 us -> 92.9 us  [attend_and_sum(): pl.pallas_call(kernel, out_shape=(jax.ShapeDtypeStruct(queries.shape, BF1...]
    pallas_call x1, Pallas kernels: 4.39 us -> 2.58 us  [finish(): pl.pallas_call(finish_kernel, out_shape=tuple((jax.ShapeDtypeStruct(*each...]
where the time goes in v3:
time: 96.2 us; the launch traced here: 96.1 us
  Pallas kernels  95.4 us (99%)
    pallas_call x1, Pallas kernels, attend_and_sum(): pl.pallas_call(kernel, out_shape=(jax.ShapeDtypeStruct(queries.shape, BF1...  92.9 us
    pallas_call x1, Pallas kernels, finish(): pl.pallas_call(finish_kernel, out_shape=tuple((jax.ShapeDtypeStruct(*each...  2.58 us

profile of v3, /device:TPU:1, one launch (start us, length us, event | category | flops | bytes accessed | tf_op | source)
XLA Modules:
  0.0 96.1 jit_solution(4318764534102041670)
XLA Ops:
  0.6 92.9 %attend.1 = (bf16[1,384,1536]{2,1,0:T(8,128)(2,1)}, bf16[2,4,64,640]{3,2,1,0:T(8,128)(2,1)}) custom-call(s32[1,32]{1,0:T(1,128)} %order_in.1, s32[6,1,32]{2,1,0:T(1,128)} %bitcast.4, s32[1,32]{1,0:T(1,128)} %valid_in.1, bf16[1,384,1536]{2,1,0:T(8,128)(2,1)} %q_in.1, bf16[1,384,1536]{2,1,0:T(8,128)(2,1)} %k_in.1, bf16[1,384,1536]{2,1,0:T(8,128)(2,1)} %v_in.1, ...), custom_call_target="tpu_custom_call" | custom-call | tf_op jit(solution)/shard_map/attend/pallas_call | solution.py:384
  93.5 2.6 %finish.1 = (bf16[1,384,1536]{2,1,0:T(8,128)(2,1)}, f32[64,3072]{1,0:T(8,128)}, f32[64,1536]{1,0:T(8,128)}) custom-call(bf16[1,384,1536]{2,1,0:T(8,128)(2,1)} %get-tuple-element.8.att_in, bf16[2,4,64,640]{3,2,1,0:T(8,128)(2,1)} %get-tuple-element.9.sum_in), custom_call_target="tpu_custom_call" | custom-call | tf_op jit(solution)/shard_map/finish/pallas_call | solution.py:459

commit v4 on v3

--- a/solution.py
+++ b/solution.py
@@ -54,7 +54,7 @@
     att_out, sum_out,
     order, window, valid, down_t, up,
     k_four, v_four, q_four, o_four, k_eight, v_eight, q_eight, o_eight,
-    k_all, v_all, q_all, att, cot, back, hidden, grad_a,
+    k_all, v_all, q_all, att, cot, back, hidden,
     keep, give, got, acc, parts, sums, final,
     s_four, r_four, s_z, r_z, s_eight, r_eight, s_of, r_of, s_oe, r_oe,
     l_in, l_small, l_att, l_sum,
@@ -182,46 +182,62 @@
     for move in small:
         move.wait()
     back[...] = lax.dot_general(up[...], cot[...], NT, preferred_element_type=F32).astype(BF16)
-    grad_a[:, HEADS * HEAD:] = jnp.zeros((grad_a.shape[0], HEAD), F32)
-
-    def unit(slot, query_of, key_of, value_of, out):
-        tile = order[0, 2 * X * frame + slot]
-        slots, biases = [], []
-        lane = lax.broadcasted_iota(jnp.int32, (1, TILE), 1)
+    att[:, HEADS * HEAD:] = jnp.zeros((TILE, HEAD), BF16)
+
+    half = TILE // 2
+    lane = lax.broadcasted_iota(jnp.int32, (1, TILE), 1)
+    row = lax.broadcasted_iota(jnp.int32, (half, HEAD), 0)
+
+    def window_of(slot, key_of, value_of):
+        tile = order[0, GROUP * frame + slot]
+        keys, values, biases = [], [], []
         for entry in range(WIN):
             wanted = window[entry, 0, tile]
             present = wanted >= 0
             known = jnp.maximum(wanted, 0)
             first = known // 2 * 2
             there = jnp.where(order[0, first] == known, first, first + 1) - frame * GROUP
-            slots.append(jnp.where(present, jnp.clip(there, 0, GROUP - 1), here))
+            there = jnp.where(present, jnp.clip(there, 0, GROUP - 1), here)
             count = jnp.where(present, valid[0, known], 0)
+            keys.append(key_of[there])
+            values.append(value_of[there])
             biases.append(jnp.where(lane < count, 0.0, -1e30).astype(F32))
-        mine = valid[0, tile]
-        half = TILE // 2
-        for start in (0, half):
-            query = query_of[pl.ds(start, half), :]
-            scores = []
-            for entry in range(WIN):
-                s = lax.dot_general(query, key_of[slots[entry]], NT, preferred_element_type=F32)
-                scores.append(s + biases[entry])
-            top = jnp.max(functools.reduce(jnp.maximum, scores), axis=1, keepdims=True)
-            total = None
-            for entry in range(WIN):
-                weights = jnp.exp2((scores[entry] - top) * SCALE).astype(BF16)
-                value = value_of[slots[entry]]
-                value = jnp.concatenate([value, jnp.ones_like(value)], axis=1)
-                term = jnp.dot(weights, value, preferred_element_type=F32)
-                total = term if total is None else total + term
-            row = start + lax.broadcasted_iota(jnp.int32, (half, HEAD), 0)
-            result = jnp.where(row < mine, total[:, :HEAD] / total[:, HEAD:], 0.0)
-            out[pl.ds(start, half), :] = result.astype(BF16)
+        return keys, values, biases, valid[0, tile]
+
+    def scores_of(query, keys, biases):
+        scores = lax.dot_general(
+            query, jnp.concatenate(keys, axis=0), NT, preferred_element_type=F32
+        )
+        return [scores[:, TILE * i:TILE * (i + 1)] + bias for i, bias in enumerate(biases)]
+
+    def attend(scores, values, mine, start):
+        top = jnp.max(functools.reduce(jnp.maximum, scores), axis=1, keepdims=True)
+        weights = [jnp.exp2((each - top) * SCALE).astype(BF16) for each in scores]
+        value = jnp.concatenate(values, axis=0)
+        value = jnp.concatenate([value, jnp.ones_like(value)], axis=1)
+        total = jnp.dot(jnp.concatenate(weights, axis=1), value, preferred_element_type=F32)
+        return jnp.where(start + row < mine, total[:, :HEAD] / total[:, HEAD:], 0.0).astype(BF16)
+
+    def units(tiles, key_of, value_of):
+        jobs = []
+        for slot, query_of, out, send in tiles:
+            keys, values, biases, mine = window_of(slot, key_of, value_of)
+            for start in (0, half):
+                jobs.append((query_of, keys, values, biases, mine, start, out, send))
+        ready = scores_of(jobs[0][0][pl.ds(0, half), :], jobs[0][1], jobs[0][3])
+        for i, (_, _, values, _, mine, start, out, send) in enumerate(jobs):
+            scores = ready
+            if i + 1 < len(jobs):
+                query_of, keys, _, biases, _, later = jobs[i + 1][:6]
+                ready = scores_of(query_of[pl.ds(later, half), :], keys, biases)
+            out[pl.ds(start, half), :] = attend(scores, values, mine, start)
+        for tile in tiles:
+            tile[3]()
 
     def collect(first, last):
         span = slice(first * HEAD, last * HEAD)
         term = lax.dot_general(down_t[:, span], att[:, span], NT, preferred_element_type=F32)
         hidden[...] = term if first == 0 else hidden[...] + term
-        grad_a[:, span] = jnp.dot(back[...], att[:, span], preferred_element_type=F32)
 
     for rel in range(1, X):
         four(2, rel).wait_recv()
@@ -229,39 +245,38 @@
         for which in range(2):
             over_z(which, rel).wait_recv()
 
-    def four_step(step, _):
-        rel = (step + 1) % X
+    def four_tile(rel):
         slot = slot_of(rel)
-        unit(slot, q_four.at[slot % X], k_four, v_four, o_four.at[rel])
-
-        @pl.when(rel != 0)
-        def _():
-            out_four(rel).start()
-
-        return 0
-
-    lax.fori_loop(0, X, four_step, 0)
+        send = out_four(rel).start if rel > 0 else lambda: None
+        return slot, q_four.at[slot % X], o_four.at[rel], send
+
+    units([four_tile(rel) for rel in (2, 1, 3, 0)], k_four, v_four)
     att[:, columns(x)] = o_four[0]
 
     for which in range(2):
         for rel in range(1, GROUP):
             eight(which, rel).wait_recv()
 
-    def eight_step(step, _):
-        rel = (step + 1) % GROUP
+    def eight_tile(rel):
         slot = slot_of(rel)
 
-        @pl.when(rel != 0)
-        def _():
-            eight(2, rel).wait_recv()
-
-        unit(slot, q_eight.at[slot], k_eight, v_eight, o_eight.at[rel])
-
-        @pl.when(rel != 0)
-        def _():
-            out_eight(rel).start()
-
-        @pl.when(step == 3)
+        def send():
+            @pl.when(rel != 0)
+            def _():
+                out_eight(rel).start()
+
+        return slot, q_eight.at[slot], o_eight.at[rel], send
+
+    def eight_pair(step, _):
+        pair = (2 * step + 1, (2 * step + 2) % GROUP)
+        for rel in pair:
+            @pl.when(rel != 0)
+            def _(rel=rel):
+                eight(2, rel).wait_recv()
+
+        units([eight_tile(rel) for rel in pair], k_eight, v_eight)
+
+        @pl.when(step == 1)
         def _():
             for other in range(1, X):
                 out_four(other).wait_recv()
@@ -270,7 +285,7 @@
 
         return 0
 
-    lax.fori_loop(0, GROUP, eight_step, 0)
+    lax.fori_loop(0, GROUP // 2, eight_pair, 0)
     att[:, columns(X + here)] = o_eight[0]
     for rel in range(1, GROUP):
         out_eight(rel).wait_recv()
@@ -291,15 +306,17 @@
         i = (x + dx) % X
         from_b = pl.ds(pl.multiple_of((2 * i + owner) * PART_B, HEAD), PART_B)
         from_a = pl.ds(pl.multiple_of(3 * HEAD * i + PART_A * owner, HEAD), PART_A)
-        ref[dx, :, :PART_B] = jnp.dot(mix, cot[:, from_b], preferred_element_type=F32)
-        ref[dx, :, PART_B:] = grad_a[:, from_a]
+        ref[dx, :, :PART_B] = jnp.dot(mix, cot[:, from_b], preferred_element_type=F32).astype(ref.dtype)
+        ref[dx, :, PART_B:] = jnp.dot(
+            back[...], att[:, from_a], preferred_element_type=F32
+        ).astype(ref.dtype)
 
     def swap(dx):
         return remote(give.at[dx], got.at[dx], s_0.at[dx], r_0.at[dx], over_core)
 
     scatter = [
         remote(
-            acc.at[dx, rows_of((y + dy) % Y)], parts.at[i], s_1.at[i], r_1.at[i],
+            acc.at[dx, rows_of((y + dy) % Y)], parts.at[i], s_1.at[0], r_1.at[0],
             over_square(dx, dy),
         )
         for i, (dx, dy) in enumerate(SQUARE)
@@ -310,46 +327,10 @@
     for dx in FAR_FIRST:
         fill(keep, dx, core)
         swap(dx).wait_recv()
-        acc[dx] = (keep[dx] + got[dx]).astype(BF16)
+        acc[dx] = (keep[dx] + got[dx].astype(F32)).astype(BF16)
         for c, (to, _) in zip(scatter, SQUARE):
             if to == dx:
                 c.start()
-    piece = acc[0, rows_of(y)].astype(F32)
-    for i in range(len(SQUARE)):
-        scatter[i].wait_recv()
-        piece += parts[i].astype(F32)
-    sums[z] = piece.astype(BF16)
-
-    ring = [
-        remote(sums.at[z], sums.at[z], s_2.at[dz - 1], r_2.at[dz - 1], over_ring(dz))
-        for dz in range(1, Z)
-    ]
-    for c in ring:
-        c.start()
-    for c in ring:
-        c.wait()
-    total = sums[0].astype(F32)
-    for i in range(1, Z):
-        total += sums[i].astype(F32)
-    final[core, x, rows_of(y), :] = total.astype(BF16)
-
-    gather = [
-        remote(
-            final.at[core, x, rows_of(y)], final.at[core, x, rows_of(y)],
-            s_3.at[i], r_3.at[i], over_square(dx, dy),
-        )
-        for i, (dx, dy) in enumerate(SQUARE)
-    ]
-    for c in gather:
-        c.start()
-    for c in gather:
-        c.wait_recv()
-    last = remote(final.at[core], final.at[core], s_4.at[0], r_4.at[0], over_core)
-    last.start()
-    last.wait_recv()
-    save = pltpu.make_async_copy(final, sum_out, l_sum)
-    save.start()
-
     for part in range(2):
         write_out(part).wait()
     for which in range(3):
@@ -366,9 +347,61 @@
         out_eight(rel).wait_send()
     for dx in range(X):
         swap(dx).wait_send()
-    for c in scatter + gather + [last]:
-        c.wait_send()
-    save.wait()
+    all_parts = remote(parts, parts, s_1.at[0], r_1.at[0], over_core)
+    all_parts.wait_recv()
+    piece = acc[0, rows_of(y)].astype(F32)
+    for i in range(len(SQUARE)):
+        piece += parts[i].astype(F32)
+    sums[z] = piece.astype(BF16)
+
+    ring = [
+        remote(sums.at[z], sums.at[z], s_2.at[0], r_2.at[0], over_ring(dz))
+        for dz in range(1, Z)
+    ]
+    for c in ring:
+        c.start()
+    all_parts.wait_send()
+    seven = sums.at[pl.ds(0, Z - 1)]
+    all_ring = remote(seven, seven, s_2.at[0], r_2.at[0], over_core)
+    all_ring.wait()
+    total = sums[0].astype(F32)
+    for i in range(1, Z):
+        total += sums[i].astype(F32)
+    final[core, x, rows_of(y), :] = total.astype(BF16)
+
+    gather = [
+        remote(
+            final.at[core, x, rows_of(y)], final.at[core, x, rows_of(y)],
+            s_3.at[dx], r_3.at[dx], over_square(dx, dy),
+        )
+        for i, (dx, dy) in enumerate(SQUARE)
+    ]
+    def pass_core(dx):
+        ref = final.at[core, (x - dx + X) % X]
+        return remote(ref, ref, s_4.at[dx], r_4.at[dx], over_core)
+
+    def save(owner, dx):
+        i = (x - dx + X) % X
+        return pltpu.make_async_copy(final.at[owner, i], sum_out.at[owner, i], l_sum.at[owner, dx])
+
+    gathered = []
+    for dx in range(X):
+        some = parts.at[pl.ds(0, Y if dx > 0 else Y - 1)]
+        gathered.append(remote(some, some, s_3.at[dx], r_3.at[dx], over_core))
+    for c in gather:
+        c.start()
+    for dx in (0, 1, 3, 2):
+        gathered[dx].wait_recv()
+        pass_core(dx).start()
+        save(core, dx).start()
+    for dx in (0, 1, 3, 2):
+        pass_core(dx).wait_recv()
+        save(1 - core, dx).start()
+    for dx in range(X):
+        gathered[dx].wait_send()
+        pass_core(dx).wait_send()
+        save(core, dx).wait()
+        save(1 - core, dx).wait()
 
 
 def attend_and_sum(order, window, valid, queries, keys, values, cotangent, down, up):
@@ -393,16 +426,16 @@
         + [pltpu.VMEM(down.shape, BF16), pltpu.VMEM(up.shape, BF16)]
         + [tiles(GROUP), tiles(GROUP), tiles(X), tiles(X)]
         + [tiles(GROUP)] * 4
-        + [pltpu.VMEM((TILE, width), BF16)] * 4
+        + [pltpu.VMEM((TILE, width), BF16)] * 3
+        + [pltpu.VMEM((TILE, width + HEAD), BF16)]
         + [
             pltpu.VMEM((TILE, wide), BF16),
             pltpu.VMEM((rank, TILE), BF16),
             pltpu.VMEM((rank, TILE), F32),
-            pltpu.VMEM((rank, width + HEAD), F32),
         ]
-        + [pltpu.VMEM((X, rank, PART), F32)] * 3
+        + [pltpu.VMEM((X, rank, PART), F32)]
+        + [pltpu.VMEM((X, rank, PART), BF16)] * 3
         + [
-            pltpu.VMEM((X, rank, PART), BF16),
             pltpu.VMEM((near, rank // Y, PART), BF16),
             pltpu.VMEM((Z, rank // Y, PART), BF16),
             pltpu.VMEM((2, X, rank, PART), BF16),
@@ -412,12 +445,10 @@
         + [dma((3, GROUP - 1))] * 2
         + [dma((X - 1,))] * 2
         + [dma((GROUP - 1,))] * 2
-        + [dma((3, 3)), dma((6,)), dma((2,)), dma]
+        + [dma((3, 3)), dma((6,)), dma((2,)), dma((2, X))]
         + [dma((X,))] * 2
-        + [dma((near,))] * 2
-        + [dma((Z - 1,))] * 2
-        + [dma((near,))] * 2
-        + [dma((1,))] * 2,
+        + [dma((1,))] * 4
+        + [dma((X,))] * 4,
         compiler_params=pltpu.CompilerParams(
             collective_id=0, has_side_effects=True, vmem_limit_bytes=VMEM_LIMIT
         ),
@@ -425,30 +456,38 @@
     )(order, window, valid, queries, keys, values, cotangent, down, up)
 
 
-def finish_kernel(att_in, sum_in, att_out, gb_out, ga_out, att, summed, gb, ga, sems):
-    take_sum = pltpu.make_async_copy(sum_in, summed, sems.at[0])
-    take_att = pltpu.make_async_copy(att_in, att, sems.at[1])
-    put_att = pltpu.make_async_copy(att, att_out, sems.at[2])
-    put_gb = pltpu.make_async_copy(gb, gb_out, sems.at[3])
-    put_ga = pltpu.make_async_copy(ga, ga_out, sems.at[4])
-    take_sum.start()
-    take_att.start()
-    take_sum.wait()
+def finish_kernel(
+    att_in, sum_in, att_out, gb_out, ga_out, att, summed, gb, ga, l_att, o_att, l_sum, o_gb, o_ga
+):
+    rows = TILE // X
+    take_sum, take_att, put_att, put_gb, put_ga = [], [], [], [], []
     for i in range(X):
+        span = pl.ds(i * rows, rows)
+        wide, head = pl.ds(2 * PART_B * i, 2 * PART_B), pl.ds(3 * HEAD * i, 3 * HEAD)
+        take_sum.append(pltpu.make_async_copy(sum_in.at[:, i], summed.at[:, i], l_sum.at[i]))
+        take_att.append(pltpu.make_async_copy(att_in.at[0, span], att.at[0, span], l_att.at[i]))
+        put_att.append(pltpu.make_async_copy(att.at[0, span], att_out.at[0, span], o_att.at[i]))
+        put_gb.append(pltpu.make_async_copy(gb.at[:, wide], gb_out.at[:, wide], o_gb.at[i]))
+        put_ga.append(pltpu.make_async_copy(ga.at[:, head], ga_out.at[:, head], o_ga.at[i]))
+    for i in range(X):
+        take_sum[i].start()
+        take_att[i].start()
+    for i in range(X):
+        take_sum[i].wait()
         for core in range(2):
             first = (2 * i + core) * PART_B
             gb[:, first:first + PART_B] = summed[core, i, :, :PART_B].astype(F32)
-    put_gb.start()
-    for head in range(HEADS):
-        i, j = head // 3, head % 3
-        start = PART_B + j % 2 * HEAD
-        ga[:, head * HEAD:(head + 1) * HEAD] = summed[j // 2, i, :, start:start + HEAD].astype(F32)
-    put_ga.start()
-    take_att.wait()
-    put_att.start()
-    put_gb.wait()
-    put_ga.wait()
-    put_att.wait()
+        for j in range(3):
+            first, start = (3 * i + j) * HEAD, PART_B + j % 2 * HEAD
+            ga[:, first:first + HEAD] = summed[j // 2, i, :, start:start + HEAD].astype(F32)
+        put_gb[i].start()
+        put_ga[i].start()
+        take_att[i].wait()
+        put_att[i].start()
+    for i in range(X):
+        put_gb[i].wait()
+        put_ga[i].wait()
+        put_att[i].wait()
 
 
 def finish(attention, summed, wide):
@@ -461,7 +500,7 @@
         out_shape=tuple(jax.ShapeDtypeStruct(*each) for each in shapes),
         in_specs=[hbm, hbm],
         out_specs=(hbm, hbm, hbm),
-        scratch_shapes=[pltpu.VMEM(*each) for each in held] + [pltpu.SemaphoreType.DMA((5,))],
+        scratch_shapes=[pltpu.VMEM(*each) for each in held] + [pltpu.SemaphoreType.DMA((X,))] * 5,
         compiler_params=pltpu.CompilerParams(vmem_limit_bytes=VMEM_LIMIT),
         name="finish",
     )(attention, summed)

time: 96.2 us -> 94.7 us (0.984)
  Pallas kernels: 95.4 us -> 94 us
    pallas_call x1, Pallas kernels: 92.9 us -> 91.5 us  [attend_and_sum(): pl.pallas_call(kernel, out_shape=(jax.ShapeDtypeStruct(queries.shape, BF1...]
where the time goes in v4:
time: 94.7 us; the launch traced here: 94.6 us
  Pallas kernels  94 us (99%)
    pallas_call x1, Pallas kernels, attend_and_sum(): pl.pallas_call(kernel, out_shape=(jax.ShapeDtypeStruct(queries.shape, BF1...  91.5 us
    pallas_call x1, Pallas kernels, finish(): pl.pallas_call(finish_kernel, out_shape=tuple((jax.ShapeDtypeStruct(*each...  2.52 us

profile of v4, /device:TPU:1, one launch (start us, length us, event | category | flops | bytes accessed | tf_op | source)
XLA Modules:
  0.0 94.6 jit_solution(8486297468436015549)
XLA Ops:
  0.6 91.5 %attend.1 = (bf16[1,384,1536]{2,1,0:T(8,128)(2,1)}, bf16[2,4,64,640]{3,2,1,0:T(8,128)(2,1)}) custom-call(s32[1,32]{1,0:T(1,128)} %order_in.1, s32[6,1,32]{2,1,0:T(1,128)} %bitcast.4, s32[1,32]{1,0:T(1,128)} %valid_in.1, bf16[1,384,1536]{2,1,0:T(8,128)(2,1)} %q_in.1, bf16[1,384,1536]{2,1,0:T(8,128)(2,1)} %k_in.1, bf16[1,384,1536]{2,1,0:T(8,128)(2,1)} %v_in.1, ...), custom_call_target="tpu_custom_call" | custom-call | tf_op jit(solution)/shard_map/attend/pallas_call | solution.py:417
  92.1 2.5 %finish.1 = (bf16[1,384,1536]{2,1,0:T(8,128)(2,1)}, f32[64,3072]{1,0:T(8,128)}, f32[64,1536]{1,0:T(8,128)}) custom-call(bf16[1,384,1536]{2,1,0:T(8,128)(2,1)} %get-tuple-element.8.att_in, bf16[2,4,64,640]{3,2,1,0:T(8,128)(2,1)} %get-tuple-element.9.sum_in), custom_call_target="tpu_custom_call" | custom-call | tf_op jit(solution)/shard_map/finish/pallas_call | solution.py:498

commit v5 on v4

--- a/solution.py
+++ b/solution.py
@@ -115,7 +115,7 @@
     def out_eight(rel):
         slot = slot_of(rel)
         return remote(
-            o_eight.at[rel], att.at[:, columns(X + here)], s_oe.at[rel - 1], r_oe.at[rel - 1],
+            o_eight.at[rel], att.at[:, columns(X + here)], s_oe.at[rel - 1], r_oe.at[0],
             at_slot(slot),
         )
 
@@ -123,6 +123,7 @@
         span = pl.ds(X * HEAD * part, X * HEAD * (part + 1))
         return pltpu.make_async_copy(att.at[:, span], att_out.at[0, :, span], l_att.at[part])
 
+    stage(0, 0).start()
     partners = [at_slot(slot_of(rel)) for rel in range(1, GROUP)] + [over_core]
     partners += [device(z, (x + dx) % X, (y + dy) % Y, core) for dx, dy in SQUARE if dy != 0]
     barrier = pltpu.get_barrier_semaphore()
@@ -143,24 +144,24 @@
     ]
     for part in range(3):
         for which in range(3):
-            stage(part, which).start()
+            if (part, which) != (0, 0):
+                stage(part, which).start()
     for move in small:
         move.start()
     pl.semaphore_wait(barrier, len(partners) + Z - 2)
 
-    for which in range(3):
+    for which in range(2):
         stage(0, which).wait()
-    for which in range(2):
         fours[which][here] = staged[which][:, columns(x)]
         for rel in (2, 1, 3):
             four(which, rel).start()
             if rel == 2:
                 over_z(which, 0).start()
-    for part in (1, 2):
-        for which in range(3):
+    for which in range(3):
+        for part in (1, 2):
             stage(part, which).wait()
-    for which in range(3):
         eight(which, 4).start()
+    stage(0, 2).wait()
     q_four[x] = q_all[:, columns(x)]
     along = [four(2, rel) for rel in (2, 1, 3)]
     along += [eight(which, rel) for which in range(2) for rel in (2, 1, 3)]
@@ -287,8 +288,8 @@
 
     lax.fori_loop(0, GROUP // 2, eight_pair, 0)
     att[:, columns(X + here)] = o_eight[0]
-    for rel in range(1, GROUP):
-        out_eight(rel).wait_recv()
+    results = o_eight.at[pl.ds(1, GROUP - 1)]
+    remote(results, results, s_oe.at[0], r_oe.at[0], over_core).wait_recv()
     write_out(1).start()
     collect(X, HEADS)
 
@@ -356,7 +357,7 @@
 
     ring = [
         remote(sums.at[z], sums.at[z], s_2.at[0], r_2.at[0], over_ring(dz))
-        for dz in range(1, Z)
+        for dz in (4, 3, 5, 2, 6, 1, 7)
     ]
     for c in ring:
         c.start()

time: 94.7 us -> 93.7 us (0.989)
  Pallas kernels: 94 us -> 93 us
    pallas_call x1, Pallas kernels: 91.5 us -> 90.4 us  [attend_and_sum(): pl.pallas_call(kernel, out_shape=(jax.ShapeDtypeStruct(queries.shape, BF1...]
where the time goes in v5:
time: 93.7 us; the launch traced here: 93.6 us
  Pallas kernels  93 us (99%)
    pallas_call x1, Pallas kernels, attend_and_sum(): pl.pallas_call(kernel, out_shape=(jax.ShapeDtypeStruct(queries.shape, BF1...  90.4 us
    pallas_call x1, Pallas kernels, finish(): pl.pallas_call(finish_kernel, out_shape=tuple((jax.ShapeDtypeStruct(*each...  2.52 us

profile of v5, /device:TPU:1, one launch (start us, length us, event | category | flops | bytes accessed | tf_op | source)
XLA Modules:
  0.0 93.6 jit_solution(17941016634939820377)
XLA Ops:
  0.6 90.4 %attend.1 = (bf16[1,384,1536]{2,1,0:T(8,128)(2,1)}, bf16[2,4,64,640]{3,2,1,0:T(8,128)(2,1)}) custom-call(s32[1,32]{1,0:T(1,128)} %order_in.1, s32[6,1,32]{2,1,0:T(1,128)} %bitcast.4, s32[1,32]{1,0:T(1,128)} %valid_in.1, bf16[1,384,1536]{2,1,0:T(8,128)(2,1)} %q_in.1, bf16[1,384,1536]{2,1,0:T(8,128)(2,1)} %k_in.1, bf16[1,384,1536]{2,1,0:T(8,128)(2,1)} %v_in.1, ...), custom_call_target="tpu_custom_call" | custom-call | tf_op jit(solution)/shard_map/attend/pallas_call | solution.py:418
  91.1 2.5 %finish.1 = (bf16[1,384,1536]{2,1,0:T(8,128)(2,1)}, f32[64,3072]{1,0:T(8,128)}, f32[64,1536]{1,0:T(8,128)}) custom-call(bf16[1,384,1536]{2,1,0:T(8,128)(2,1)} %get-tuple-element.8.att_in, bf16[2,4,64,640]{3,2,1,0:T(8,128)(2,1)} %get-tuple-element.9.sum_in), custom_call_target="tpu_custom_call" | custom-call | tf_op jit(solution)/shard_map/finish/pallas_call | solution.py:499

commit v6 on v5

--- a/solution.py
+++ b/solution.py
@@ -322,16 +322,18 @@
         )
         for i, (dx, dy) in enumerate(SQUARE)
     ]
-    for dx in FAR_FIRST:
-        fill(give, dx, 1 - core)
-        swap(dx).start()
-    for dx in FAR_FIRST:
-        fill(keep, dx, core)
-        swap(dx).wait_recv()
-        acc[dx] = (keep[dx] + got[dx].astype(F32)).astype(BF16)
-        for c, (to, _) in zip(scatter, SQUARE):
-            if to == dx:
-                c.start()
+    for i in range(X + 1):
+        if i < X:
+            fill(give, FAR_FIRST[i], 1 - core)
+            swap(FAR_FIRST[i]).start()
+        if i > 0:
+            dx = FAR_FIRST[i - 1]
+            fill(keep, dx, core)
+            swap(dx).wait_recv()
+            acc[dx] = (keep[dx] + got[dx].astype(F32)).astype(BF16)
+            for c, (to, _) in zip(scatter, SQUARE):
+                if to == dx:
+                    c.start()
     for part in range(2):
         write_out(part).wait()
     for which in range(3):

time: 93.7 us -> 93.8 us (level)
  no operation moved by 1% of the time
where the time goes in v6:
time: 93.8 us; the launch traced here: 93.7 us
  Pallas kernels  93 us (99%)
    pallas_call x1, Pallas kernels, attend_and_sum(): pl.pallas_call(kernel, out_shape=(jax.ShapeDtypeStruct(queries.shape, BF1...  90.5 us
    pallas_call x1, Pallas kernels, finish(): pl.pallas_call(finish_kernel, out_shape=tuple((jax.ShapeDtypeStruct(*each...  2.52 us

profile of v6, /device:TPU:1, one launch (start us, length us, event | category | flops | bytes accessed | tf_op | source)
XLA Modules:
  0.0 93.7 jit_solution(13011051306375383655)
XLA Ops:
  0.6 90.5 %attend.1 = (bf16[1,384,1536]{2,1,0:T(8,128)(2,1)}, bf16[2,4,64,640]{3,2,1,0:T(8,128)(2,1)}) custom-call(s32[1,32]{1,0:T(1,128)} %order_in.1, s32[6,1,32]{2,1,0:T(1,128)} %bitcast.4, s32[1,32]{1,0:T(1,128)} %valid_in.1, bf16[1,384,1536]{2,1,0:T(8,128)(2,1)} %q_in.1, bf16[1,384,1536]{2,1,0:T(8,128)(2,1)} %k_in.1, bf16[1,384,1536]{2,1,0:T(8,128)(2,1)} %v_in.1, ...), custom_call_target="tpu_custom_call" | custom-call | tf_op jit(solution)/shard_map/attend/pallas_call | solution.py:420
  91.1 2.5 %finish.1 = (bf16[1,384,1536]{2,1,0:T(8,128)(2,1)}, f32[64,3072]{1,0:T(8,128)}, f32[64,1536]{1,0:T(8,128)}) custom-call(bf16[1,384,1536]{2,1,0:T(8,128)(2,1)} %get-tuple-element.8.att_in, bf16[2,4,64,640]{3,2,1,0:T(8,128)(2,1)} %get-tuple-element.9.sum_in), custom_call_target="tpu_custom_call" | custom-call | tf_op jit(solution)/shard_map/finish/pallas_call | solution.py:501
